TPU v7x, 512 devices: a whole 4x8x8 slice. The times are simulated.
512 devices in a mesh: section: 2 (over x_lo), row: 16 (over y, core), col: 16 (over z, x_hi).
Axes of the slice: x: 4 (x_hi: 2, x_lo: 2; x = x_hi * 2 + x_lo), y: 8, z: 8, core: 2. Of those that a mesh axis runs over, the one named last changes fastest.
Arguments:
- activations: bfloat16 [2, 512, 6144], P('section', 'col', 'row'), may hold values from -6 to 6
- weights: bfloat16 [2, 6144, 24576], P('section', 'row', 'col'), may hold values from -0.078125 to 0.078125
Outputs:
- boundary: bfloat16 [2, 512, 6144], P('section', 'col', 'row')
- weight_grads: bfloat16 [2, 6144, 24576], P('section', 'row', 'col')
All inputs are finite; a program needn't handle non-finite values.
Results may differ from a plain program's by a relative error of at most 0.034.
Values may be sent and summed in bfloat16 or wider, within the bound.
No kernel may reach another device: no remote copies, remote signals or barrier semaphores. Data moves between devices by JAX's collectives and lax.ppermute only.
A program may use at most 64 MiB of HBM per device.

v0:
```python
import jax
import jax.numpy as jnp
from jax import lax
from jax.sharding import PartitionSpec as P

gelu_scale = 0.7978845608028654
cubic_coef = 0.044715


def from_partner(block, axis, distance):
    count = lax.axis_size(axis)
    route = []
    for low in range(count):
        high = low | 1 << distance
        if high != low and high < count:
            route += [(low, high), (high, low)]
    return lax.ppermute(block, axis, route)


def gelu_value(preact):
    inner = gelu_scale * (preact + cubic_coef * preact * preact * preact)
    return 0.5 * preact * (1.0 + jnp.tanh(inner))


def gelu_slope(preact):
    inner = gelu_scale * (preact + cubic_coef * preact * preact * preact)
    tangent = jnp.tanh(inner)
    return 0.5 * (1.0 + tangent) + 0.5 * preact * (1.0 - tangent * tangent) * gelu_scale * (
        1.0 + 3.0 * cubic_coef * preact * preact
    )


def per_device(activations, weights):
    panel = activations[0]
    weight = weights[0]
    leading = lax.axis_index("section") == 0
    gathered = lax.all_gather(panel, "col", axis=0, tiled=True)
    rows_part = gathered
    shares = lax.psum_scatter(
        jnp.dot(rows_part, weight, preferred_element_type=jnp.float32).astype(jnp.bfloat16),
        "row",
        scatter_dimension=0,
        tiled=True,
    ).astype(jnp.float32)
    sending = jnp.where(leading, gelu_value(shares), shares).astype(jnp.bfloat16)
    partner = from_partner(sending, "section", 0)
    received = partner.astype(jnp.float32)
    own_side = jnp.where(leading, received * gelu_slope(shares), received).astype(jnp.bfloat16)
    hidden_side = lax.all_gather(own_side, "row", axis=0, tiled=True)
    weight_grad = lax.dot_general(
        gathered, hidden_side, (((0,), (0,)), ((), ())), preferred_element_type=jnp.float32
    ).astype(jnp.bfloat16)
    rows_part = hidden_side
    result = lax.psum_scatter(
        lax.dot_general(
            rows_part, weight, (((1,), (1,)), ((), ())), preferred_element_type=jnp.float32
        ).astype(jnp.bfloat16),
        "col",
        scatter_dimension=0,
        tiled=True,
    )
    return (result[None], weight_grad[None])


def solution(mesh):
    placed = (P("section", "col", "row"), P("section", "row", "col"))
    return jax.shard_map(
        per_device,
        mesh=mesh,
        in_specs=placed,
        out_specs=(P("section", "col", "row"), P("section", "row", "col")),
        check_vma=False,
    )
```

profile of v0, /device:TPU:1, one launch (start us, length us, event | category | flops | bytes accessed | tf_op | source)
XLA Modules:
  0.0 377.9 jit_solution(10393410455991783571)
XLA Ops:
  7.2 0.0 copy-start
  7.2 0.0 reduce-scatter.3.cloned.1.call-start
  7.2 43.1 %all-gather = bf16[1,512,384]{2,1,0:T(8,128)(2,1)S(1)} all-gather(bf16[1,32,384]{2,1,0:T(8,128)(2,1)} %param.2), channel_id=2, replica_groups=mesh['section'=2,'row'=16,'col'=16] {'col'}, dimensions={1}, use_global_device_ids=true | all-gather | bytes 417792 | tf_op jit(solution)/shard_map/all_gather | solution.py:37
  50.3 0.0 copy-done
  50.3 2.1 convolution_convert_fusion
  52.5 0.0 reduce-scatter.3.cloned.1.call-update
  52.5 0.0 all-gather.3.cloned.1.call-start
  52.5 60.3 %reduce-scatter.3.cloned.1.call-done = bf16[32,1536]{1,0:T(8,128)(2,1)} async-done(((bf16[512,1536]{1,0:T(8,128)(2,1)}), bf16[32,1536]{1,0:T(8,128)(2,1)}) %reduce-scatter.3.cloned.1.call-update) | async-done | bytes 98320 | tf_op jit(solution)/shard_map/reduce_scatter | solution.py:39
  112.9 1.0 fusion.13
  113.9 2.1 collective-permute-start
  116.0 3.2 collective-permute-done
  119.2 1.7 fusion.10
  120.9 0.0 all-gather.3.cloned.1.call-update
  120.9 0.0 reduce-scatter.5.cloned.1.call-start
  121.0 44.0 %all-gather.3.cloned.1.call-done = bf16[512,1536]{1,0:T(8,128)(2,1)} async-done(((bf16[32,1536]{1,0:T(8,128)(2,1)}), bf16[512,1536]{1,0:T(8,128)(2,1)}) %all-gather.3.cloned.1.call-update) | async-done | bytes 1572880 | tf_op jit(solution)/shard_map/all_gather | solution.py:49
  165.0 3.2 convolution_convert_fusion.2
  168.1 0.0 reduce-scatter.5.cloned.1.call-update
  168.1 2.4 fusion
  170.6 1.5 copy.4
  172.0 199.4 %reduce-scatter.5.cloned.1.call-done = bf16[32,384]{1,0:T(8,128)(2,1)} async-done(((bf16[512,384]{1,0:T(8,128)(2,1)}), bf16[32,384]{1,0:T(8,128)(2,1)}) %reduce-scatter.5.cloned.1.call-update) | async-done | bytes 24592 | tf_op jit(solution)/shard_map/reduce_scatter | solution.py:54
Async XLA Ops:
  7.2 43.2 %copy-start = (bf16[1,384,1536]{2,1,0:T(8,128)(2,1)S(1)}, bf16[1,384,1536]{2,1,0:T(8,128)(2,1)}, u32[]{:S(2)}) copy-start(bf16[1,384,1536]{2,1,0:T(8,128)(2,1)} %param.3) | copy-start | bytes 3538948
  7.2 105.7 %reduce-scatter.3.cloned.1.call-start = ((), (), s32[]{:S(2)}) async-start(), calls=%async_computation.2 | async-start | bytes 1671168 | tf_op jit(solution)/shard_map/reduce_scatter | solution.py:39
  52.5 112.5 %all-gather.3.cloned.1.call-start = ((), (), s32[]{:S(2)}) async-start(), calls=%async_computation.3 | async-start | bytes 1671168 | tf_op jit(solution)/shard_map/all_gather | solution.py:49
  113.9 5.4 %collective-permute-start = (bf16[32,1536]{1,0:T(8,128)(2,1)S(1)}, bf16[32,1536]{1,0:T(8,128)(2,1)S(1)}, u32[]{:S(2)}, u32[]{:S(2)}) collective-permute-start(bf16[32,1536]{1,0:T(8,128)(2,1)S(1)} %fusion.13), channel_id=1, source_target_pairs={{0,256},{256,0},{1,257},{257,1},{2,258},{258,2},{3,259},{259,3},{4... | collective-permute-start | bytes 294920 | tf_op jit(solution)/shard_map/ppermute | solution.py:17
  120.9 250.4 %reduce-scatter.5.cloned.1.call-start = ((), (), s32[]{:S(2)}) async-start(), calls=%async_computation.4 | async-start | bytes 417792 | tf_op jit(solution)/shard_map/reduce_scatter | solution.py:54
Sparse Core Ops, SparseCore 0:
  52.6 60.2 reduce-scatter.2
  121.0 43.8 all-gather.2
  170.6 200.7 reduce-scatter.4
where the time goes:
time: 382 us; the launch traced here: 378 us
  waiting for transfers between devices  307 us (80%)
  blocking collectives  43.1 us (11%)
  between operations  13.8 us (4%)
  matrix products  7.71 us (2%)
    reduce_scatter x1, waiting for transfers between devices, per_device(): lax.psum_scatter(lax.dot_general(rows_part, weight, (((1,), (1,)), ((), (...  199 us
    reduce_scatter x1, waiting for transfers between devices, per_device(): lax.psum_scatter(jnp.dot(rows_part, weight, preferred_element_type=jnp.fl...  60.3 us
    all_gather x1, waiting for transfers between devices, per_device(): hidden_side = lax.all_gather(own_side, 'row', axis=0, tiled=True)  44 us
    all_gather x1, blocking collectives, per_device(): gathered = lax.all_gather(panel, 'col', axis=0, tiled=True)  43.1 us
  transfers between devices with their start and end apart: 4, of which 4 were waited for; matrix products, arithmetic and copies ran while one was open for 1% of the time, Pallas kernels for 0%

commit v1 on v0

v1 whole, which is shorter than its diff:
```python
import jax
import jax.numpy as jnp
from jax import lax
from jax.sharding import Mesh
from jax.sharding import PartitionSpec as P

gelu_scale = 0.7978845608028654
cubic_coef = 0.044715
f32 = jnp.float32
bf16 = jnp.bfloat16


def gelu_value(preact):
    inner = gelu_scale * (preact + cubic_coef * preact * preact * preact)
    return 0.5 * preact * (1.0 + jnp.tanh(inner))


def gelu_slope(preact):
    inner = gelu_scale * (preact + cubic_coef * preact * preact * preact)
    tangent = jnp.tanh(inner)
    return 0.5 * (1.0 + tangent) + 0.5 * preact * (1.0 - tangent * tangent) * gelu_scale * (
        1.0 + 3.0 * cubic_coef * preact * preact
    )


def swap(block, axis):
    return lax.ppermute(block, axis, [(0, 1), (1, 0)])


def gather_by_exchange(block, axes):
    count = lax.axis_size(axes)
    copies = jnp.broadcast_to(block[None], (count, *block.shape))
    return lax.all_to_all(copies, axes, 0, 0).reshape(-1, block.shape[1])


def sum_by_exchange(parts, axes):
    count = lax.axis_size(axes)
    blocks = parts.reshape(count, -1, parts.shape[1])
    return lax.all_to_all(blocks, axes, 0, 0).astype(f32).sum(0)


def per_device(activations, weights):
    panel = activations[0]
    weight = weights[0]
    leading = lax.axis_index("section") == 0
    core = lax.axis_index("core")
    gathered = gather_by_exchange(panel, ("z", "x_hi"))
    half = gathered.shape[0] // 2
    own_rows = lax.dynamic_slice_in_dim(gathered, core * half, half, 0)
    other_rows = lax.dynamic_slice_in_dim(gathered, (1 - core) * half, half, 0)

    other_part = jnp.dot(other_rows, weight, preferred_element_type=f32).astype(bf16)
    arrived = swap(other_part, "core")
    own_part = jnp.dot(own_rows, weight, preferred_element_type=f32)
    chip_part = (own_part + arrived.astype(f32)).astype(bf16)
    shares = sum_by_exchange(chip_part, "y")

    sending = jnp.where(leading, gelu_value(shares), shares).astype(bf16)
    received = swap(sending, "section").astype(f32)
    own_side = jnp.where(leading, received * gelu_slope(shares), received).astype(bf16)

    own_hidden = lax.all_gather(own_side, "y", axis=0, tiled=True)
    other_hidden = swap(own_hidden, "core")

    def boundary_part(hidden):
        return lax.dot_general(hidden, weight, (((1,), (1,)), ((), ())), preferred_element_type=f32).astype(bf16)

    def grad_part(rows, hidden):
        return lax.dot_general(rows, hidden, (((0,), (0,)), ((), ())), preferred_element_type=f32)

    own_result = boundary_part(own_hidden)
    own_grad = grad_part(own_rows, own_hidden)
    other_result = boundary_part(other_hidden)
    first = core == 0
    partial = jnp.concatenate(
        [jnp.where(first, own_result, other_result), jnp.where(first, other_result, own_result)], axis=0
    )
    result = sum_by_exchange(partial, ("z", "x_hi")).astype(bf16)
    weight_grad = (own_grad + grad_part(other_rows, other_hidden)).astype(bf16)
    return (result[None], weight_grad[None])


def solution(mesh):
    sections, rows, cols = mesh.devices.shape
    fine = Mesh(
        mesh.devices.reshape(sections, rows // 2, 2, cols // 2, 2), ("section", "y", "core", "z", "x_hi")
    )
    by_token = P("section", ("z", "x_hi"), ("y", "core"))
    by_weight = P("section", ("y", "core"), ("z", "x_hi"))
    return jax.shard_map(
        per_device,
        mesh=fine,
        in_specs=(by_token, by_weight),
        out_specs=(by_token, by_weight),
        check_vma=False,
    )
```

time: 382 us -> 128 us (0.34)
  waiting for transfers between devices: 307 us -> 58.9 us
  starting transfers between devices: 2.25 us -> 38.7 us
  blocking collectives: 43.1 us -> 20.5 us
  between operations: 13.8 us -> 0.73 us
    reduce_scatter x2 -> x0, waiting for transfers between devices: 260 us -> none  [the longest x1 199 us: per_device(): lax.psum_scatter(lax.dot_general(rows_part, weight, (((1,), (1,)), ((), (...]
    all_to_all x0 -> x3, waiting for transfers between devices: none -> 51.6 us  [the longest x2 36.8 us: sum_by_exchange(): return lax.all_to_all(blocks, axes, 0, 0).astype(f32).sum(0)]
    all_gather x1 -> x0, waiting for transfers between devices: 44 us -> none  [per_device(): hidden_side = lax.all_gather(own_side, 'row', axis=0, tiled=True)]
    all_to_all x0 -> x3, starting transfers between devices: none -> 23.8 us  [the longest x1 13.4 us: gather_by_exchange(): return lax.all_to_all(copies, axes, 0, 0).reshape(-1, block.shape[1])]
    all_gather x1, blocking collectives: 43.1 us -> 20.5 us  [per_device(): own_hidden = lax.all_gather(own_side, 'y', axis=0, tiled=True)]
    ppermute x1 -> x3, starting transfers between devices: 2.13 us -> 14.9 us  [swap(): return lax.ppermute(block, axis, [(0, 1), (1, 0)])]
    ppermute x1 -> x3, waiting for transfers between devices: 3.23 us -> 7.32 us  [swap(): return lax.ppermute(block, axis, [(0, 1), (1, 0)])]
    dot_general x3 -> x6, matrix products: 7.71 us -> 5.21 us  [the longest x2 2.02 us: grad_part(): lax.dot_general(rows, hidden, (((0,), (0,)), ((), ())), preferred_element...]
  transfers between devices with their start and end apart: 4 -> 6, of which waited for: 4 -> 6; matrix products, arithmetic and copies ran while one was open for 1% -> 2% of each run, Pallas kernels for 0% -> 0%
where the time goes in v1:
time: 128 us; the launch traced here: 127 us
  waiting for transfers between devices  58.9 us (46%)
  starting transfers between devices  38.7 us (30%)
  blocking collectives  20.5 us (16%)
  matrix products  5.21 us (4%)
  other arithmetic  1.78 us (1%)
  local copies, waits for them, and re-layouts  1.62 us (1%)
    all_to_all x2, waiting for transfers between devices, sum_by_exchange(): return lax.all_to_all(blocks, axes, 0, 0).astype(f32).sum(0)  36.8 us
    all_gather x1, blocking collectives, per_device(): own_hidden = lax.all_gather(own_side, 'y', axis=0, tiled=True)  20.5 us
    ppermute x3, starting transfers between devices, swap(): return lax.ppermute(block, axis, [(0, 1), (1, 0)])  14.9 us
    all_to_all x1, waiting for transfers between devices, gather_by_exchange(): return lax.all_to_all(copies, axes, 0, 0).reshape(-1, block.shape[1])  14.8 us
    all_to_all x1, starting transfers between devices, gather_by_exchange(): return lax.all_to_all(copies, axes, 0, 0).reshape(-1, block.shape[1])  13.4 us
    all_to_all x2, starting transfers between devices, sum_by_exchange(): return lax.all_to_all(blocks, axes, 0, 0).astype(f32).sum(0)  10.4 us
    ppermute x3, waiting for transfers between devices, swap(): return lax.ppermute(block, axis, [(0, 1), (1, 0)])  7.32 us
  transfers between devices with their start and end apart: 6, of which 6 were waited for; matrix products, arithmetic and copies ran while one was open for 2% of the time, Pallas kernels for 0%

profile of v1, /device:TPU:1, one launch (start us, length us, event | category | flops | bytes accessed | tf_op | source)
XLA Modules:
  0.0 127.4 jit_solution(6790116109102812845)
XLA Ops:
  0.6 0.0 copy-start
  0.6 1.6 %broadcast_in_dim.14 = bf16[16,32,384]{2,1,0:T(8,128)(2,1)} broadcast(bf16[32,384]{1,0:T(8,128)(2,1)} %bitcast.32), dimensions={1,2} | broadcast | bytes 417792 | tf_op jit(solution)/shard_map/broadcast_in_dim | solution.py:32
  2.3 13.4 %all-to-all-start = ((bf16[16,32,384]{2,1,0:T(8,128)(2,1)}), bf16[16,32,384]{2,1,0:T(8,128)(2,1)S(1)}, u32[]{:S(2)}, u32[]{:S(2)}) async-start(bf16[16,32,384]{2,1,0:T(8,128)(2,1)} %broadcast_in_dim.14), calls=%async_computation | async-start | bytes 786432 | tf_op jit(solution)/shard_map/all_to_all | solution.py:33
  15.7 14.8 %all-to-all-done = bf16[16,32,384]{2,1,0:T(8,128)(2,1)S(1)} async-done(((bf16[16,32,384]{2,1,0:T(8,128)(2,1)}), bf16[16,32,384]{2,1,0:T(8,128)(2,1)S(1)}, u32[]{:S(2)}, u32[]{:S(2)}) %all-to-all-start) | async-done | bytes 393248 | tf_op jit(solution)/shard_map/all_to_all | solution.py:33
  30.5 0.0 copy-done
  30.5 0.6 convolution_convert_fusion
  31.1 4.0 %collective-permute-start = (bf16[256,1536]{1,0:T(8,128)(2,1)S(1)}, bf16[256,1536]{1,0:T(8,128)(2,1)S(1)}, u32[]{:S(2)}, u32[]{:S(2)}) collective-permute-start(bf16[256,1536]{1,0:T(8,128)(2,1)S(1)} %convolution_convert_fusion), channel_id=1, source_target_pairs={{0,16},{16,0},{1,17},{17,1},{2,18},{18,2},{3,19},{19,3},{4,20},{20... | collective-permute-start | bytes 2359304 | tf_op jit(solution)/shard_map/ppermute | solution.py:27
  35.1 1.9 %collective-permute-done = bf16[256,1536]{1,0:T(8,128)(2,1)S(1)} collective-permute-done((bf16[256,1536]{1,0:T(8,128)(2,1)S(1)}, bf16[256,1536]{1,0:T(8,128)(2,1)S(1)}, u32[]{:S(2)}, u32[]{:S(2)}) %collective-permute-start) | collective-permute-done | bytes 786464 | tf_op jit(solution)/shard_map/ppermute | solution.py:27
  37.0 1.4 %add_convert_fusion = bf16[256,1536]{1,0:T(8,128)(2,1)} fusion(bf16[256,1536]{1,0:T(8,128)(2,1)S(1)} %collective-permute-done, bf16[1,384,1536]{2,1,0:T(8,128)(2,1)S(1)} %copy-done, bf16[512,384]{1,0:T(8,128)(2,1)S(1)} %bitcast.29, s32[]{:T(128)S(6)} %select_n.32), kind=kOutput, calls=%fused_computation.5 | convolution fusion | flops 303169536 | bytes 2949124 | tf_op jit(solution)/shard_map/dot_general | solution.py:54
  38.5 6.8 %all-to-all-start.1 = ((bf16[8,32,1536]{2,1,0:T(8,128)(2,1)}), bf16[8,32,1536]{2,1,0:T(8,128)(2,1)S(1)}, u32[]{:S(2)}, u32[]{:S(2)}) async-start(bf16[8,32,1536]{2,1,0:T(8,128)(2,1)} %bitcast.3), calls=%async_computation.1 | async-start | bytes 1572864 | tf_op jit(solution)/shard_map/all_to_all | solution.py:39
  45.3 23.6 %all-to-all-done.1 = bf16[8,32,1536]{2,1,0:T(8,128)(2,1)S(1)} async-done(((bf16[8,32,1536]{2,1,0:T(8,128)(2,1)}), bf16[8,32,1536]{2,1,0:T(8,128)(2,1)S(1)}, u32[]{:S(2)}, u32[]{:S(2)}) %all-to-all-start.1) | async-done | bytes 786464 | tf_op jit(solution)/shard_map/all_to_all | solution.py:39
  68.9 0.1 convert_reduce_fusion
  69.0 0.1 select_convert_fusion
  69.1 2.2 %collective-permute-start.1 = (bf16[32,1536]{1,0:T(8,128)(2,1)S(1)}, bf16[32,1536]{1,0:T(8,128)(2,1)S(1)}, u32[]{:S(2)}, u32[]{:S(2)}) collective-permute-start(bf16[32,1536]{1,0:T(8,128)(2,1)S(1)} %select_convert_fusion), channel_id=1, source_target_pairs={{0,256},{256,0},{1,257},{257,1},{2,258},{258,2},{3,259},{259,3},{4... | collective-permute-start | bytes 294920 | tf_op jit(solution)/shard_map/ppermute | solution.py:27
  71.3 3.5 %collective-permute-done.1 = bf16[32,1536]{1,0:T(8,128)(2,1)S(1)} collective-permute-done((bf16[32,1536]{1,0:T(8,128)(2,1)S(1)}, bf16[32,1536]{1,0:T(8,128)(2,1)S(1)}, u32[]{:S(2)}, u32[]{:S(2)}) %collective-permute-start.1) | collective-permute-done | bytes 98336 | tf_op jit(solution)/shard_map/ppermute | solution.py:27
  74.8 0.1 fusion.22
  75.0 20.5 %all_gather.3 = bf16[256,1536]{1,0:T(8,128)(2,1)S(1)} all-gather(bf16[32,1536]{1,0:T(8,128)(2,1)S(1)} %fusion.22), channel_id=1, replica_groups=mesh['section'=2,'y'=8,'core'=2,'z'=8,'x_hi'=2] {'y'}, dimensions={0}, use_global_device_ids=true | all-gather | bytes 884736 | tf_op jit(solution)/shard_map/all_gather | solution.py:62
  95.5 8.6 %collective-permute-start.2 = (bf16[256,1536]{1,0:T(8,128)(2,1)S(1)}, bf16[256,1536]{1,0:T(8,128)(2,1)S(1)}, u32[]{:S(2)}, u32[]{:S(2)}) collective-permute-start(bf16[256,1536]{1,0:T(8,128)(2,1)S(1)} %all_gather.3), channel_id=1, source_target_pairs={{0,16},{16,0},{1,17},{17,1},{2,18},{18,2},{3,19},{19,3},{4,20},{20... | collective-permute-start | bytes 2359304 | tf_op jit(solution)/shard_map/ppermute | solution.py:27
  104.1 1.9 %collective-permute-done.2 = bf16[256,1536]{1,0:T(8,128)(2,1)S(1)} collective-permute-done((bf16[256,1536]{1,0:T(8,128)(2,1)S(1)}, bf16[256,1536]{1,0:T(8,128)(2,1)S(1)}, u32[]{:S(2)}, u32[]{:S(2)}) %collective-permute-start.2) | collective-permute-done | bytes 786464 | tf_op jit(solution)/shard_map/ppermute | solution.py:27
  106.0 0.6 fusion.14
  106.6 0.6 broadcast_select_fusion.1
  107.2 0.8 pad_maximum_fusion
  108.0 3.6 %all-to-all-start.2 = ((bf16[16,32,384]{2,1,0:T(8,128)(2,1)}), bf16[16,32,384]{2,1,0:T(8,128)(2,1)S(1)}, u32[]{:S(2)}, u32[]{:S(2)}) async-start(bf16[16,32,384]{2,1,0:T(8,128)(2,1)} %bitcast.4), calls=%async_computation.2 | async-start | bytes 786432 | tf_op jit(solution)/shard_map/all_to_all | solution.py:39
  111.6 0.5 fusion.23
  112.1 1.5 %fusion.1 = bf16[1,384,1536]{2,1,0:T(8,128)(2,1)} fusion(f32[384,1536]{1,0:T(8,128)S(1)} %fusion.23, bf16[256,1536]{1,0:T(8,128)(2,1)S(1)} %all_gather.3, bf16[512,384]{1,0:T(8,128)(2,1)S(1)} %bitcast.31, s32[]{:T(128)S(6)} %select_n.32), kind=kOutput, calls=%fused_computation.2 | convolution fusion | flops 303169536 | bytes 4521988 | tf_op jit(solution)/shard_map/dot_general | solution.py:69
  113.6 13.2 %all-to-all-done.2 = bf16[16,32,384]{2,1,0:T(8,128)(2,1)S(1)} async-done(((bf16[16,32,384]{2,1,0:T(8,128)(2,1)}), bf16[16,32,384]{2,1,0:T(8,128)(2,1)S(1)}, u32[]{:S(2)}, u32[]{:S(2)}) %all-to-all-start.2) | async-done | bytes 393248 | tf_op jit(solution)/shard_map/all_to_all | solution.py:39
  126.8 0.7 reduce_sum.22
Async XLA Ops:
  0.6 29.9 %copy-start = (bf16[1,384,1536]{2,1,0:T(8,128)(2,1)S(1)}, bf16[1,384,1536]{2,1,0:T(8,128)(2,1)}, u32[]{:S(2)}) copy-start(bf16[1,384,1536]{2,1,0:T(8,128)(2,1)} %param.3) | copy-start | bytes 3538948
  2.3 28.2 %all-to-all-start = ((bf16[16,32,384]{2,1,0:T(8,128)(2,1)}), bf16[16,32,384]{2,1,0:T(8,128)(2,1)S(1)}, u32[]{:S(2)}, u32[]{:S(2)}) async-start(bf16[16,32,384]{2,1,0:T(8,128)(2,1)} %broadcast_in_dim.14), calls=%async_computation | async-start | bytes 786432 | tf_op jit(solution)/shard_map/all_to_all | solution.py:33
  31.1 5.9 %collective-permute-start = (bf16[256,1536]{1,0:T(8,128)(2,1)S(1)}, bf16[256,1536]{1,0:T(8,128)(2,1)S(1)}, u32[]{:S(2)}, u32[]{:S(2)}) collective-permute-start(bf16[256,1536]{1,0:T(8,128)(2,1)S(1)} %convolution_convert_fusion), channel_id=1, source_target_pairs={{0,16},{16,0},{1,17},{17,1},{2,18},{18,2},{3,19},{19,3},{4,20},{20... | collective-permute-start | bytes 2359304 | tf_op jit(solution)/shard_map/ppermute | solution.py:27
  38.5 30.4 %all-to-all-start.1 = ((bf16[8,32,1536]{2,1,0:T(8,128)(2,1)}), bf16[8,32,1536]{2,1,0:T(8,128)(2,1)S(1)}, u32[]{:S(2)}, u32[]{:S(2)}) async-start(bf16[8,32,1536]{2,1,0:T(8,128)(2,1)} %bitcast.3), calls=%async_computation.1 | async-start | bytes 1572864 | tf_op jit(solution)/shard_map/all_to_all | solution.py:39
  69.1 5.8 %collective-permute-start.1 = (bf16[32,1536]{1,0:T(8,128)(2,1)S(1)}, bf16[32,1536]{1,0:T(8,128)(2,1)S(1)}, u32[]{:S(2)}, u32[]{:S(2)}) collective-permute-start(bf16[32,1536]{1,0:T(8,128)(2,1)S(1)} %select_convert_fusion), channel_id=1, source_target_pairs={{0,256},{256,0},{1,257},{257,1},{2,258},{258,2},{3,259},{259,3},{4... | collective-permute-start | bytes 294920 | tf_op jit(solution)/shard_map/ppermute | solution.py:27
  95.5 10.5 %collective-permute-start.2 = (bf16[256,1536]{1,0:T(8,128)(2,1)S(1)}, bf16[256,1536]{1,0:T(8,128)(2,1)S(1)}, u32[]{:S(2)}, u32[]{:S(2)}) collective-permute-start(bf16[256,1536]{1,0:T(8,128)(2,1)S(1)} %all_gather.3), channel_id=1, source_target_pairs={{0,16},{16,0},{1,17},{17,1},{2,18},{18,2},{3,19},{19,3},{4,20},{20... | collective-permute-start | bytes 2359304 | tf_op jit(solution)/shard_map/ppermute | solution.py:27
  108.0 18.8 %all-to-all-start.2 = ((bf16[16,32,384]{2,1,0:T(8,128)(2,1)}), bf16[16,32,384]{2,1,0:T(8,128)(2,1)S(1)}, u32[]{:S(2)}, u32[]{:S(2)}) async-start(bf16[16,32,384]{2,1,0:T(8,128)(2,1)} %bitcast.4), calls=%async_computation.2 | async-start | bytes 786432 | tf_op jit(solution)/shard_map/all_to_all | solution.py:39

commit v2 on v1

--- a/solution.py
+++ b/solution.py
@@ -42,7 +42,6 @@
 def per_device(activations, weights):
     panel = activations[0]
     weight = weights[0]
-    leading = lax.axis_index("section") == 0
     core = lax.axis_index("core")
     gathered = gather_by_exchange(panel, ("z", "x_hi"))
     half = gathered.shape[0] // 2
@@ -53,13 +52,14 @@
     arrived = swap(other_part, "core")
     own_part = jnp.dot(own_rows, weight, preferred_element_type=f32)
     chip_part = (own_part + arrived.astype(f32)).astype(bf16)
-    shares = sum_by_exchange(chip_part, "y")
-
-    sending = jnp.where(leading, gelu_value(shares), shares).astype(bf16)
-    received = swap(sending, "section").astype(f32)
-    own_side = jnp.where(leading, received * gelu_slope(shares), received).astype(bf16)
-
-    own_hidden = lax.all_gather(own_side, "y", axis=0, tiled=True)
+    pairs = lax.axis_size("y")
+    blocks = lax.all_to_all(chip_part.reshape(2 * pairs, -1, chip_part.shape[1]), ("section", "y"), 0, 0)
+    preact = blocks[:pairs].astype(f32).sum(0)
+    dhidden = blocks[pairs:].astype(f32).sum(0).astype(bf16).astype(f32)
+    hidden = gelu_value(preact).astype(bf16)
+    dpre = (dhidden * gelu_slope(preact)).astype(bf16)
+    sending = jnp.concatenate([jnp.broadcast_to(side[None], (pairs, *side.shape)) for side in (dpre, hidden)], axis=0)
+    own_hidden = lax.all_to_all(sending, ("section", "y"), 0, 0).reshape(half, -1)
     other_hidden = swap(own_hidden, "core")
 
     def boundary_part(hidden):

time: 128 us -> 119 us (0.930); the launches traced: 127 us -> 117 us
  blocking collectives: 20.5 us -> 52 us
  waiting for transfers between devices: 58.9 us -> 31.1 us
  starting transfers between devices: 38.7 us -> 25.6 us
    all_to_all x0 -> x2, blocking collectives: none -> 52 us  [the longest x1 26.9 us: per_device(): lax.all_to_all(chip_part.reshape(2 * pairs, -1, chip_part.shape[1]), ('se...]
    all_to_all x2 -> x1, waiting for transfers between devices: 36.8 us -> 13.1 us  [sum_by_exchange(): return lax.all_to_all(blocks, axes, 0, 0).astype(f32).sum(0)]
    all_gather x1 -> x0, blocking collectives: 20.5 us -> none  [per_device(): own_hidden = lax.all_gather(own_side, 'y', axis=0, tiled=True)]
    all_to_all x2 -> x1, starting transfers between devices: 10.4 us -> 3.55 us  [sum_by_exchange(): return lax.all_to_all(blocks, axes, 0, 0).astype(f32).sum(0)]
    ppermute x3 -> x2, starting transfers between devices: 14.9 us -> 8.65 us  [swap(): return lax.ppermute(block, axis, [(0, 1), (1, 0)])]
    ppermute x3 -> x2, waiting for transfers between devices: 7.32 us -> 3.18 us  [swap(): return lax.ppermute(block, axis, [(0, 1), (1, 0)])]
  transfers between devices with their start and end apart: 6 -> 4, of which waited for: 6 -> 4; matrix products, arithmetic and copies ran while one was open for 2% -> 2% of each run, Pallas kernels for 0% -> 0%
where the time goes in v2:
time: 119 us; the launch traced here: 117 us
  blocking collectives  52 us (44%)
  waiting for transfers between devices  31.1 us (26%)
  starting transfers between devices  25.6 us (22%)
  matrix products  4.33 us (4%)
  other arithmetic  1.7 us (1%)
  local copies, waits for them, and re-layouts  1.68 us (1%)
    all_to_all x1, blocking collectives, per_device(): lax.all_to_all(chip_part.reshape(2 * pairs, -1, chip_part.shape[1]), ('se...  26.9 us
    all_to_all x1, blocking collectives, per_device(): lax.all_to_all(sending, ('section', 'y'), 0, 0).reshape(half, -1)  25.1 us
    all_to_all x1, waiting for transfers between devices, gather_by_exchange(): return lax.all_to_all(copies, axes, 0, 0).reshape(-1, block.shape[1])  14.8 us
    all_to_all x1, starting transfers between devices, gather_by_exchange(): return lax.all_to_all(copies, axes, 0, 0).reshape(-1, block.shape[1])  13.4 us
    all_to_all x1, waiting for transfers between devices, sum_by_exchange(): return lax.all_to_all(blocks, axes, 0, 0).astype(f32).sum(0)  13.1 us
    ppermute x2, starting transfers between devices, swap(): return lax.ppermute(block, axis, [(0, 1), (1, 0)])  8.65 us
    all_to_all x1, starting transfers between devices, sum_by_exchange(): return lax.all_to_all(blocks, axes, 0, 0).astype(f32).sum(0)  3.55 us
    ppermute x2, waiting for transfers between devices, swap(): return lax.ppermute(block, axis, [(0, 1), (1, 0)])  3.18 us
  transfers between devices with their start and end apart: 4, of which 4 were waited for; matrix products, arithmetic and copies ran while one was open for 2% of the time, Pallas kernels for 0%

profile of v2, /device:TPU:1, one launch (start us, length us, event | category | flops | bytes accessed | tf_op | source)
XLA Modules:
  0.0 117.2 jit_solution(3406373822350837709)
XLA Ops:
  0.6 0.0 copy-start
  0.6 1.6 %broadcast_in_dim.26 = bf16[16,32,384]{2,1,0:T(8,128)(2,1)} broadcast(bf16[32,384]{1,0:T(8,128)(2,1)} %bitcast.37), dimensions={1,2} | broadcast | bytes 417792 | tf_op jit(solution)/shard_map/broadcast_in_dim | solution.py:32
  2.3 13.4 %all-to-all-start = ((bf16[16,32,384]{2,1,0:T(8,128)(2,1)}), bf16[16,32,384]{2,1,0:T(8,128)(2,1)S(1)}, u32[]{:S(2)}, u32[]{:S(2)}) async-start(bf16[16,32,384]{2,1,0:T(8,128)(2,1)} %broadcast_in_dim.26), calls=%async_computation | async-start | bytes 786432 | tf_op jit(solution)/shard_map/all_to_all | solution.py:33
  15.7 14.8 %all-to-all-done = bf16[16,32,384]{2,1,0:T(8,128)(2,1)S(1)} async-done(((bf16[16,32,384]{2,1,0:T(8,128)(2,1)}), bf16[16,32,384]{2,1,0:T(8,128)(2,1)S(1)}, u32[]{:S(2)}, u32[]{:S(2)}) %all-to-all-start) | async-done | bytes 393248 | tf_op jit(solution)/shard_map/all_to_all | solution.py:33
  30.5 0.0 copy-done
  30.5 0.6 convolution_convert_fusion
  31.1 4.0 %collective-permute-start = (bf16[256,1536]{1,0:T(8,128)(2,1)S(1)}, bf16[256,1536]{1,0:T(8,128)(2,1)S(1)}, u32[]{:S(2)}, u32[]{:S(2)}) collective-permute-start(bf16[256,1536]{1,0:T(8,128)(2,1)S(1)} %convolution_convert_fusion), channel_id=1, source_target_pairs={{0,16},{16,0},{1,17},{17,1},{2,18},{18,2},{3,19},{19,3},{4,20},{20... | collective-permute-start | bytes 2359304 | tf_op jit(solution)/shard_map/ppermute | solution.py:27
  35.1 1.9 %collective-permute-done = bf16[256,1536]{1,0:T(8,128)(2,1)S(1)} collective-permute-done((bf16[256,1536]{1,0:T(8,128)(2,1)S(1)}, bf16[256,1536]{1,0:T(8,128)(2,1)S(1)}, u32[]{:S(2)}, u32[]{:S(2)}) %collective-permute-start) | collective-permute-done | bytes 786464 | tf_op jit(solution)/shard_map/ppermute | solution.py:27
  37.0 0.6 add_convert_fusion
  37.6 26.9 %all_to_all.20 = bf16[16,16,1536]{2,1,0:T(8,128)(2,1)S(1)} all-to-all(bf16[16,16,1536]{2,1,0:T(8,128)(2,1)S(1)} %bitcast.36), channel_id=1, replica_groups=mesh['section'=2,'y'=8,'core'=2,'z'=8,'x_hi'=2] {'section','y'}, dimensions={0} | all-to-all | bytes 1572864 | tf_op jit(solution)/shard_map/all_to_all | solution.py:56
  64.4 0.1 slice_reduce_fusion
  64.5 0.1 convert_reduce_fusion
  64.6 0.1 fusion.28
  64.7 0.1 pad_maximum_fusion
  64.8 25.1 %all_to_all.21 = bf16[16,16,1536]{2,1,0:T(8,128)(2,1)S(1)} all-to-all(bf16[16,16,1536]{2,1,0:T(8,128)(2,1)S(1)} %pad_maximum_fusion), channel_id=1, replica_groups=mesh['section'=2,'y'=8,'core'=2,'z'=8,'x_hi'=2] {'section','y'}, dimensions={0} | all-to-all | bytes 1572864 | tf_op jit(solution)/shard_map/all_to_all | solution.py:62
  89.9 4.6 %collective-permute-start.1 = (bf16[256,1536]{1,0:T(8,128)(2,1)S(1)}, bf16[256,1536]{1,0:T(8,128)(2,1)S(1)}, u32[]{:S(2)}, u32[]{:S(2)}) collective-permute-start(bf16[256,1536]{1,0:T(8,128)(2,1)S(1)} %bitcast.33), channel_id=1, source_target_pairs={{0,16},{16,0},{1,17},{17,1},{2,18},{18,2},{3,19},{19,3},{4,20},{20... | collective-permute-start | bytes 2359304 | tf_op jit(solution)/shard_map/ppermute | solution.py:27
  94.6 0.6 fusion.11
  95.1 1.3 %collective-permute-done.1 = bf16[256,1536]{1,0:T(8,128)(2,1)S(1)} collective-permute-done((bf16[256,1536]{1,0:T(8,128)(2,1)S(1)}, bf16[256,1536]{1,0:T(8,128)(2,1)S(1)}, u32[]{:S(2)}, u32[]{:S(2)}) %collective-permute-start.1) | collective-permute-done | bytes 786464 | tf_op jit(solution)/shard_map/ppermute | solution.py:27
  96.4 0.6 broadcast_select_fusion.1
  97.0 0.8 pad_maximum_fusion.1
  97.8 3.6 %all-to-all-start.3 = ((bf16[16,32,384]{2,1,0:T(8,128)(2,1)}), bf16[16,32,384]{2,1,0:T(8,128)(2,1)S(1)}, u32[]{:S(2)}, u32[]{:S(2)}) async-start(bf16[16,32,384]{2,1,0:T(8,128)(2,1)} %bitcast.5), calls=%async_computation.3 | async-start | bytes 786432 | tf_op jit(solution)/shard_map/all_to_all | solution.py:39
  101.4 0.5 fusion.19
  101.9 1.5 %fusion.1 = bf16[1,384,1536]{2,1,0:T(8,128)(2,1)} fusion(f32[384,1536]{1,0:T(8,128)S(1)} %fusion.19, bf16[256,1536]{1,0:T(8,128)(2,1)S(1)} %collective-permute-done.1, bf16[512,384]{1,0:T(8,128)(2,1)S(1)} %bitcast.32, s32[]{:T(128)S(6)} %select_n.20), kind=kOutput, calls=%fused_computation.2 | convolution fusion | flops 303169536 | bytes 4521988 | tf_op jit(solution)/shard_map/dot_general | solution.py:69
  103.4 13.1 %all-to-all-done.3 = bf16[16,32,384]{2,1,0:T(8,128)(2,1)S(1)} async-done(((bf16[16,32,384]{2,1,0:T(8,128)(2,1)}), bf16[16,32,384]{2,1,0:T(8,128)(2,1)S(1)}, u32[]{:S(2)}, u32[]{:S(2)}) %all-to-all-start.3) | async-done | bytes 393248 | tf_op jit(solution)/shard_map/all_to_all | solution.py:39
  116.5 0.7 reduce_sum.35
  (2 shorter events, 0.1 us)
Async XLA Ops:
  0.6 29.9 %copy-start = (bf16[1,384,1536]{2,1,0:T(8,128)(2,1)S(1)}, bf16[1,384,1536]{2,1,0:T(8,128)(2,1)}, u32[]{:S(2)}) copy-start(bf16[1,384,1536]{2,1,0:T(8,128)(2,1)} %param.3) | copy-start | bytes 3538948
  2.3 28.2 %all-to-all-start = ((bf16[16,32,384]{2,1,0:T(8,128)(2,1)}), bf16[16,32,384]{2,1,0:T(8,128)(2,1)S(1)}, u32[]{:S(2)}, u32[]{:S(2)}) async-start(bf16[16,32,384]{2,1,0:T(8,128)(2,1)} %broadcast_in_dim.26), calls=%async_computation | async-start | bytes 786432 | tf_op jit(solution)/shard_map/all_to_all | solution.py:33
  31.1 5.9 %collective-permute-start = (bf16[256,1536]{1,0:T(8,128)(2,1)S(1)}, bf16[256,1536]{1,0:T(8,128)(2,1)S(1)}, u32[]{:S(2)}, u32[]{:S(2)}) collective-permute-start(bf16[256,1536]{1,0:T(8,128)(2,1)S(1)} %convolution_convert_fusion), channel_id=1, source_target_pairs={{0,16},{16,0},{1,17},{17,1},{2,18},{18,2},{3,19},{19,3},{4,20},{20... | collective-permute-start | bytes 2359304 | tf_op jit(solution)/shard_map/ppermute | solution.py:27
  89.9 6.5 %collective-permute-start.1 = (bf16[256,1536]{1,0:T(8,128)(2,1)S(1)}, bf16[256,1536]{1,0:T(8,128)(2,1)S(1)}, u32[]{:S(2)}, u32[]{:S(2)}) collective-permute-start(bf16[256,1536]{1,0:T(8,128)(2,1)S(1)} %bitcast.33), channel_id=1, source_target_pairs={{0,16},{16,0},{1,17},{17,1},{2,18},{18,2},{3,19},{19,3},{4,20},{20... | collective-permute-start | bytes 2359304 | tf_op jit(solution)/shard_map/ppermute | solution.py:27
  97.8 18.7 %all-to-all-start.3 = ((bf16[16,32,384]{2,1,0:T(8,128)(2,1)}), bf16[16,32,384]{2,1,0:T(8,128)(2,1)S(1)}, u32[]{:S(2)}, u32[]{:S(2)}) async-start(bf16[16,32,384]{2,1,0:T(8,128)(2,1)} %bitcast.5), calls=%async_computation.3 | async-start | bytes 786432 | tf_op jit(solution)/shard_map/all_to_all | solution.py:39

commit v3 on v2

v3 whole, which is shorter than its diff:
```python
import jax
import jax.numpy as jnp
from jax import lax
from jax.sharding import Mesh
from jax.sharding import PartitionSpec as P

gelu_scale = 0.7978845608028654
cubic_coef = 0.044715
f32 = jnp.float32
bf16 = jnp.bfloat16
every_axis = ("section", "y", "core", "z", "x_hi")
chip_cols = ("core", "z", "x_hi")
lead = ("section", "y")


def gelu_value(preact):
    inner = gelu_scale * (preact + cubic_coef * preact * preact * preact)
    return 0.5 * preact * (1.0 + jnp.tanh(inner))


def gelu_slope(preact):
    inner = gelu_scale * (preact + cubic_coef * preact * preact * preact)
    tangent = jnp.tanh(inner)
    return 0.5 * (1.0 + tangent) + 0.5 * preact * (1.0 - tangent * tangent) * gelu_scale * (
        1.0 + 3.0 * cubic_coef * preact * preact
    )


def swap(block, axis):
    return lax.ppermute(block, axis, [(0, 1), (1, 0)])


def dot(left, right):
    return jnp.dot(left, right, preferred_element_type=f32)


def dot_t(left, right):
    return lax.dot_general(left, right, (((1,), (1,)), ((), ())), preferred_element_type=f32)


def grad_dot(rows, hidden):
    return lax.dot_general(rows, hidden, (((0,), (0,)), ((), ())), preferred_element_type=f32)


def per_device(activations, weights):
    panel = activations[0]
    weight = weights[0]
    core = lax.axis_index("core")
    cols = lax.axis_size("z") * lax.axis_size("x_hi")
    pairs = lax.axis_size("y")
    share = panel.shape[0] // 2
    width = panel.shape[1]

    out_panels = jnp.broadcast_to(panel.reshape(2, 1, share, width), (2, cols, share, width))
    gathered = lax.all_to_all(out_panels.reshape(2 * cols, share, width), chip_cols, 0, 0).reshape(2, cols * share, width)
    step = weight.shape[0] // 3
    both = jnp.concatenate([lax.all_gather(weight[at * step : (at + 1) * step], "core") for at in range(3)], axis=1)
    chip_part = (dot(gathered[0], both[0]) + dot(gathered[1], both[1])).astype(bf16)

    blocks = lax.all_to_all(chip_part.reshape(2 * pairs, -1, chip_part.shape[1]), lead, 0, 0)
    preact = blocks[:pairs].astype(f32).sum(0)
    dhidden = blocks[pairs:].astype(f32).sum(0).astype(bf16).astype(f32)
    hidden = gelu_value(preact).astype(bf16)
    dpre = (dhidden * gelu_slope(preact)).astype(bf16)
    sending = jnp.concatenate([jnp.broadcast_to(side[None], (pairs, *side.shape)) for side in (dpre, hidden)], axis=0)
    side = lax.all_to_all(sending, lead, 0, 0).reshape(cols * share, -1)

    partial = jnp.stack([dot_t(side, both[at]).astype(bf16) for at in range(2)])
    arrived = lax.all_to_all(partial.reshape(2 * cols, share, width), chip_cols, 0, 0)

    late_gathered, late_side = lax.optimization_barrier((gathered, side))
    late_own = lax.dynamic_index_in_dim(late_gathered, core, 0, False)
    late_other = swap(lax.dynamic_index_in_dim(late_gathered, 1 - core, 0, False), "core")
    rows = late_side.shape[0] // 2
    other_side = jnp.concatenate([swap(late_side[at * rows : (at + 1) * rows], "core") for at in range(2)], axis=0)
    weight_grad = (grad_dot(late_own, late_side) + grad_dot(late_other, other_side)).astype(bf16)
    arrived, weight_grad = lax.optimization_barrier((arrived, weight_grad))
    result = arrived.reshape(2, cols, share, width).astype(f32).sum(1).astype(bf16).reshape(2 * share, width)
    return (result[None], weight_grad[None])


def solution(mesh):
    sections, rows, cols = mesh.devices.shape
    fine = Mesh(mesh.devices.reshape(sections, rows // 2, 2, cols // 2, 2), every_axis)
    by_token = P("section", ("z", "x_hi"), ("y", "core"))
    by_weight = P("section", ("y", "core"), ("z", "x_hi"))
    return jax.shard_map(
        per_device,
        mesh=fine,
        in_specs=(by_token, by_weight),
        out_specs=(by_token, by_weight),
        check_vma=False,
    )
```

time: 119 us -> 112 us (0.941)
  blocking collectives: 52 us -> 34.1 us
  starting transfers between devices: 25.6 us -> 33.6 us
  local copies, waits for them, and re-layouts: 1.68 us -> 3.17 us
  waiting for transfers between devices: 31.1 us -> 32.5 us
    all_to_all x2 -> x1, blocking collectives: 52 us -> 27 us  [per_device(): lax.all_to_all(chip_part.reshape(2 * pairs, -1, chip_part.shape[1]), lead...]
    all_to_all x2 -> x3, starting transfers between devices: 17 us -> 27.1 us  [the longest x1 14.4 us: per_device(): lax.all_to_all(out_panels.reshape(2 * cols, share, width), chip_cols, 0, 0)]
    all_gather x0 -> x3, blocking collectives: none -> 7.08 us  [per_device(): lax.all_gather(weight[at * step:(at + 1) * step], 'core')]
    all_to_all x2 -> x3, waiting for transfers between devices: 27.9 us -> 31.8 us  [the longest x1 19.7 us: per_device(): side = lax.all_to_all(sending, lead, 0, 0).reshape(cols * share, -1)]
    ppermute x2 -> x3, waiting for transfers between devices: 3.18 us -> 0.69 us  [swap(): return lax.ppermute(block, axis, [(0, 1), (1, 0)])]
    ppermute x2 -> x3, starting transfers between devices: 8.65 us -> 6.46 us  [swap(): return lax.ppermute(block, axis, [(0, 1), (1, 0)])]
    slice x0 -> x3, local copies, waits for them, and re-layouts: none -> 1.41 us  [the longest x1 1.31 us: per_device(): weight[at * step:(at + 1) * step]]
  transfers between devices with their start and end apart: 4 -> 6, of which waited for: 4 -> 4; matrix products, arithmetic and copies ran while one was open for 2% -> 3% of each run, Pallas kernels for 0% -> 0%
where the time goes in v3:
time: 112 us; the launch traced here: 111 us
  blocking collectives  34.1 us (30%)
  starting transfers between devices  33.6 us (30%)
  waiting for transfers between devices  32.5 us (29%)
  matrix products  4.35 us (4%)
  local copies, waits for them, and re-layouts  3.17 us (3%)
  other arithmetic  2.6 us (2%)
    all_to_all x1, blocking collectives, per_device(): lax.all_to_all(chip_part.reshape(2 * pairs, -1, chip_part.shape[1]), lead...  27 us
    all_to_all x1, waiting for transfers between devices, per_device(): side = lax.all_to_all(sending, lead, 0, 0).reshape(cols * share, -1)  19.7 us
    all_to_all x1, starting transfers between devices, per_device(): lax.all_to_all(out_panels.reshape(2 * cols, share, width), chip_cols, 0, 0)  14.4 us
    all_gather x3, blocking collectives, per_device(): lax.all_gather(weight[at * step:(at + 1) * step], 'core')  7.08 us
    all_to_all x1, starting transfers between devices, per_device(): lax.all_to_all(partial.reshape(2 * cols, share, width), chip_cols, 0, 0)  6.84 us
    ppermute x3, starting transfers between devices, swap(): return lax.ppermute(block, axis, [(0, 1), (1, 0)])  6.46 us
    all_to_all x1, waiting for transfers between devices, per_device(): lax.all_to_all(out_panels.reshape(2 * cols, share, width), chip_cols, 0, 0)  6.41 us
    all_to_all x1, starting transfers between devices, per_device(): side = lax.all_to_all(sending, lead, 0, 0).reshape(cols * share, -1)  5.82 us
  transfers between devices with their start and end apart: 6, of which 4 were waited for; matrix products, arithmetic and copies ran while one was open for 3% of the time, Pallas kernels for 0%

profile of v3, /device:TPU:1, one launch (start us, length us, event | category | flops | bytes accessed | tf_op | source)
XLA Modules:
  0.0 111.1 jit_solution(4173439308323473515)
XLA Ops:
  0.6 1.5 %broadcast_in_dim.11 = bf16[2,16,16,384]{3,2,1,0:T(8,128)(2,1)} broadcast(bf16[2,16,384]{2,1,0:T(8,128)(2,1)} %bitcast.47), dimensions={0,2,3} | broadcast | bytes 417792 | tf_op jit(solution)/shard_map/broadcast_in_dim | solution.py:54
  2.1 14.4 %all-to-all-start = ((bf16[32,16,384]{2,1,0:T(8,128)(2,1)}), bf16[32,16,384]{2,1,0:T(8,128)(2,1)S(1)}, u32[]{:S(2)}, u32[]{:S(2)}) async-start(bf16[32,16,384]{2,1,0:T(8,128)(2,1)} %bitcast.2), calls=%async_computation | async-start | bytes 786432 | tf_op jit(solution)/shard_map/all_to_all | solution.py:55
  16.6 1.3 %fusion.20 = (bf16[1,128,1536]{2,1,0:T(8,128)(2,1)S(1)}, bf16[1,128,1536]{2,1,0:T(8,128)(2,1)S(1)}, bf16[1,128,1536]{2,1,0:T(8,128)(2,1)S(1)}) fusion(bf16[1,384,1536]{2,1,0:T(8,128)(2,1)} %param.3), kind=kLoop, calls=%fused_computation.38 | loop fusion | bytes 2359296 | tf_op jit(solution)/shard_map/slice | solution.py:57
  17.9 2.4 %all_gather.12 = bf16[2,128,1536]{2,1,0:T(8,128)(2,1)S(1)} all-gather(bf16[1,128,1536]{2,1,0:T(8,128)(2,1)S(1)} %get-tuple-element.11), channel_id=1, replica_groups=mesh['section'=2,'y'=8,'core'=2,'z'=8,'x_hi'=2] {'core'}, dimensions={0}, use_global_device_ids=true | all-gather | bytes 1179648 | tf_op jit(solution)/shard_map/all_gather | solution.py:57
  20.3 2.4 %all_gather.13 = bf16[2,128,1536]{2,1,0:T(8,128)(2,1)S(1)} all-gather(bf16[1,128,1536]{2,1,0:T(8,128)(2,1)S(1)} %get-tuple-element.12), channel_id=1, replica_groups=mesh['section'=2,'y'=8,'core'=2,'z'=8,'x_hi'=2] {'core'}, dimensions={0}, use_global_device_ids=true | all-gather | bytes 1179648 | tf_op jit(solution)/shard_map/all_gather | solution.py:57
  22.6 2.4 %all_gather.14 = bf16[2,128,1536]{2,1,0:T(8,128)(2,1)S(1)} all-gather(bf16[1,128,1536]{2,1,0:T(8,128)(2,1)S(1)} %get-tuple-element.10), channel_id=1, replica_groups=mesh['section'=2,'y'=8,'core'=2,'z'=8,'x_hi'=2] {'core'}, dimensions={0}, use_global_device_ids=true | all-gather | bytes 1179648 | tf_op jit(solution)/shard_map/all_gather | solution.py:57
  25.0 0.1 constant_dynamic-update-slice_fusion.2
  25.1 0.1 constant_dynamic-update-slice_fusion.1
  25.1 0.1 constant_dynamic-update-slice_fusion
  25.2 6.4 %all-to-all-done = bf16[32,16,384]{2,1,0:T(8,128)(2,1)S(1)} async-done(((bf16[32,16,384]{2,1,0:T(8,128)(2,1)}), bf16[32,16,384]{2,1,0:T(8,128)(2,1)S(1)}, u32[]{:S(2)}, u32[]{:S(2)}) %all-to-all-start) | async-done | bytes 393248 | tf_op jit(solution)/shard_map/all_to_all | solution.py:55
  31.6 0.6 fusion.4
  32.2 0.6 fusion.1
  32.8 27.0 %all_to_all.20 = bf16[16,16,1536]{2,1,0:T(8,128)(2,1)S(1)} all-to-all(bf16[16,16,1536]{2,1,0:T(8,128)(2,1)S(1)} %bitcast.43), channel_id=1, replica_groups=mesh['section'=2,'y'=8,'core'=2,'z'=8,'x_hi'=2] {'section','y'}, dimensions={0} | all-to-all | bytes 1572864 | tf_op jit(solution)/shard_map/all_to_all | solution.py:60
  59.8 0.1 convert_reduce_fusion
  59.8 0.1 slice_reduce_fusion
  59.9 0.1 fusion.17
  60.1 0.9 pad_maximum_fusion
  61.0 5.8 %all-to-all-start.2 = ((bf16[16,16,1536]{2,1,0:T(8,128)(2,1)}), bf16[16,16,1536]{2,1,0:T(8,128)(2,1)S(1)}, u32[]{:S(2)}, u32[]{:S(2)}) async-start(bf16[16,16,1536]{2,1,0:T(8,128)(2,1)} %pad_maximum_fusion), calls=%async_computation.2 | async-start | bytes 1572864 | tf_op jit(solution)/shard_map/all_to_all | solution.py:66
  66.9 19.7 %all-to-all-done.2 = bf16[16,16,1536]{2,1,0:T(8,128)(2,1)S(1)} async-done(((bf16[16,16,1536]{2,1,0:T(8,128)(2,1)}), bf16[16,16,1536]{2,1,0:T(8,128)(2,1)S(1)}, u32[]{:S(2)}, u32[]{:S(2)}) %all-to-all-start.2) | async-done | bytes 786464 | tf_op jit(solution)/shard_map/all_to_all | solution.py:66
  86.6 0.6 fusion.3
  87.2 0.6 fusion.2
  87.8 0.8 pad_maximum_fusion.1
  88.6 6.8 %all-to-all-start.3 = ((bf16[32,16,384]{2,1,0:T(8,128)(2,1)}), bf16[32,16,384]{2,1,0:T(8,128)(2,1)S(1)}, u32[]{:S(2)}, u32[]{:S(2)}) async-start(bf16[32,16,384]{2,1,0:T(8,128)(2,1)} %bitcast.11), calls=%async_computation.3 | async-start | bytes 786432 | tf_op jit(solution)/shard_map/all_to_all | solution.py:69
  95.4 0.1 fusion.21
  95.5 2.1 %collective-permute-start.2 = (bf16[128,1536]{1,0:T(8,128)(2,1)S(1)}, bf16[128,1536]{1,0:T(8,128)(2,1)S(1)}, u32[]{:S(2)}, u32[]{:S(2)}) collective-permute-start(bf16[128,1536]{1,0:T(8,128)(2,1)S(1)} %get-tuple-element.14), channel_id=1, source_target_pairs={{0,16},{16,0},{1,17},{17,1},{2,18},{18,2},{3,19},{19,3},{4,20},{20... | collective-permute-start | bytes 1179656 | tf_op jit(solution)/shard_map/ppermute | solution.py:30
  97.6 2.2 %collective-permute-start.1 = (bf16[128,1536]{1,0:T(8,128)(2,1)S(1)}, bf16[128,1536]{1,0:T(8,128)(2,1)S(1)}, u32[]{:S(2)}, u32[]{:S(2)}) collective-permute-start(bf16[128,1536]{1,0:T(8,128)(2,1)S(1)} %get-tuple-element.13), channel_id=1, source_target_pairs={{0,16},{16,0},{1,17},{17,1},{2,18},{18,2},{3,19},{19,3},{4,20},{20... | collective-permute-start | bytes 1179656 | tf_op jit(solution)/shard_map/ppermute | solution.py:30
  99.8 2.1 %collective-permute-start = (bf16[256,384]{1,0:T(8,128)(2,1)S(1)}, bf16[256,384]{1,0:T(8,128)(2,1)S(1)}, u32[]{:S(2)}, u32[]{:S(2)}) collective-permute-start(bf16[256,384]{1,0:T(8,128)(2,1)S(1)} %dynamic-slice_bitcast_fusion), channel_id=1, source_target_pairs={{0,16},{16,0},{1,17},{17,1},{2,18},{18,2},{3,19},{19,3},{4,20},{20... | collective-permute-start | bytes 589832 | tf_op jit(solution)/shard_map/ppermute | solution.py:30
  102.0 0.5 fusion.8
  102.5 0.7 collective-permute-done
  103.2 0.0 collective-permute-done.2
  103.2 0.0 collective-permute-done.1
  103.2 1.5 %fusion = bf16[384,1536]{1,0:T(8,128)(2,1)} fusion(f32[384,1536]{1,0:T(8,128)S(1)} %fusion.8, bf16[256,384]{1,0:T(8,128)(2,1)S(1)} %collective-permute-done, bf16[128,1536]{1,0:T(8,128)(2,1)S(1)} %collective-permute-done.2, bf16[128,1536]{1,0:T(8,128)(2,1)S(1)} %collective-permute-done.1), kind=kOutput, calls=%fused_computation.1 | convolution fusion | flops 304742400 | bytes 4521984 | tf_op jit(solution)/shard_map/dot_general | solution.py:42
  104.7 5.7 %all-to-all-done.3 = bf16[32,16,384]{2,1,0:T(8,128)(2,1)S(1)} async-done(((bf16[32,16,384]{2,1,0:T(8,128)(2,1)}), bf16[32,16,384]{2,1,0:T(8,128)(2,1)S(1)}, u32[]{:S(2)}, u32[]{:S(2)}) %all-to-all-start.3) | async-done | bytes 393248 | tf_op jit(solution)/shard_map/all_to_all | solution.py:69
  110.4 0.7 bitcast_reduce_fusion
  (4 shorter events, 0.1 us)
Async XLA Ops:
  2.1 29.4 %all-to-all-start = ((bf16[32,16,384]{2,1,0:T(8,128)(2,1)}), bf16[32,16,384]{2,1,0:T(8,128)(2,1)S(1)}, u32[]{:S(2)}, u32[]{:S(2)}) async-start(bf16[32,16,384]{2,1,0:T(8,128)(2,1)} %bitcast.2), calls=%async_computation | async-start | bytes 786432 | tf_op jit(solution)/shard_map/all_to_all | solution.py:55
  61.0 25.6 %all-to-all-start.2 = ((bf16[16,16,1536]{2,1,0:T(8,128)(2,1)}), bf16[16,16,1536]{2,1,0:T(8,128)(2,1)S(1)}, u32[]{:S(2)}, u32[]{:S(2)}) async-start(bf16[16,16,1536]{2,1,0:T(8,128)(2,1)} %pad_maximum_fusion), calls=%async_computation.2 | async-start | bytes 1572864 | tf_op jit(solution)/shard_map/all_to_all | solution.py:66
  88.6 21.8 %all-to-all-start.3 = ((bf16[32,16,384]{2,1,0:T(8,128)(2,1)}), bf16[32,16,384]{2,1,0:T(8,128)(2,1)S(1)}, u32[]{:S(2)}, u32[]{:S(2)}) async-start(bf16[32,16,384]{2,1,0:T(8,128)(2,1)} %bitcast.11), calls=%async_computation.3 | async-start | bytes 786432 | tf_op jit(solution)/shard_map/all_to_all | solution.py:69
  95.5 7.7 %collective-permute-start.2 = (bf16[128,1536]{1,0:T(8,128)(2,1)S(1)}, bf16[128,1536]{1,0:T(8,128)(2,1)S(1)}, u32[]{:S(2)}, u32[]{:S(2)}) collective-permute-start(bf16[128,1536]{1,0:T(8,128)(2,1)S(1)} %get-tuple-element.14), channel_id=1, source_target_pairs={{0,16},{16,0},{1,17},{17,1},{2,18},{18,2},{3,19},{19,3},{4,20},{20... | collective-permute-start | bytes 1179656 | tf_op jit(solution)/shard_map/ppermute | solution.py:30
  97.6 5.6 %collective-permute-start.1 = (bf16[128,1536]{1,0:T(8,128)(2,1)S(1)}, bf16[128,1536]{1,0:T(8,128)(2,1)S(1)}, u32[]{:S(2)}, u32[]{:S(2)}) collective-permute-start(bf16[128,1536]{1,0:T(8,128)(2,1)S(1)} %get-tuple-element.13), channel_id=1, source_target_pairs={{0,16},{16,0},{1,17},{17,1},{2,18},{18,2},{3,19},{19,3},{4,20},{20... | collective-permute-start | bytes 1179656 | tf_op jit(solution)/shard_map/ppermute | solution.py:30
  99.8 3.3 %collective-permute-start = (bf16[256,384]{1,0:T(8,128)(2,1)S(1)}, bf16[256,384]{1,0:T(8,128)(2,1)S(1)}, u32[]{:S(2)}, u32[]{:S(2)}) collective-permute-start(bf16[256,384]{1,0:T(8,128)(2,1)S(1)} %dynamic-slice_bitcast_fusion), channel_id=1, source_target_pairs={{0,16},{16,0},{1,17},{17,1},{2,18},{18,2},{3,19},{19,3},{4,20},{20... | collective-permute-start | bytes 589832 | tf_op jit(solution)/shard_map/ppermute | solution.py:30

commit v4 on v3

--- a/solution.py
+++ b/solution.py
@@ -45,9 +45,10 @@
 def per_device(activations, weights):
     panel = activations[0]
     weight = weights[0]
-    core = lax.axis_index("core")
+    core = lax.axis_index("core").astype(jnp.uint32)
     cols = lax.axis_size("z") * lax.axis_size("x_hi")
     pairs = lax.axis_size("y")
+    panel, core, other_core = lax.optimization_barrier((panel, core, 1 - core))
     share = panel.shape[0] // 2
     width = panel.shape[1]
 
@@ -65,12 +66,13 @@
     sending = jnp.concatenate([jnp.broadcast_to(side[None], (pairs, *side.shape)) for side in (dpre, hidden)], axis=0)
     side = lax.all_to_all(sending, lead, 0, 0).reshape(cols * share, -1)
 
-    partial = jnp.stack([dot_t(side, both[at]).astype(bf16) for at in range(2)])
+    partial = lax.dot_general(both, side, (((2,), (1,)), ((), ())), preferred_element_type=f32).astype(bf16).transpose(0, 2, 1)
     arrived = lax.all_to_all(partial.reshape(2 * cols, share, width), chip_cols, 0, 0)
 
     late_gathered, late_side = lax.optimization_barrier((gathered, side))
-    late_own = lax.dynamic_index_in_dim(late_gathered, core, 0, False)
-    late_other = swap(lax.dynamic_index_in_dim(late_gathered, 1 - core, 0, False), "core")
+    late_own = lax.dynamic_slice(late_gathered, (core, jnp.uint32(0), jnp.uint32(0)), (1, *late_gathered.shape[1:]))[0]
+    late_other = lax.dynamic_slice(late_gathered, (other_core, jnp.uint32(0), jnp.uint32(0)), (1, *late_gathered.shape[1:]))[0]
+    late_other = swap(late_other, "core")
     rows = late_side.shape[0] // 2
     other_side = jnp.concatenate([swap(late_side[at * rows : (at + 1) * rows], "core") for at in range(2)], axis=0)
     weight_grad = (grad_dot(late_own, late_side) + grad_dot(late_other, other_side)).astype(bf16)

time: 112 us -> 110 us (0.982)
  blocking collectives: 34.1 us -> 59.8 us
  waiting for transfers between devices: 32.5 us -> 12.8 us
  starting transfers between devices: 33.6 us -> 27.6 us
  other arithmetic: 2.6 us -> 0.92 us
    all_to_all x0 -> x1, blocking collectives: none -> 25.8 us  [per_device(): side = lax.all_to_all(sending, lead, 0, 0).reshape(cols * share, -1)]
    all_to_all x1 -> x0, waiting for transfers between devices: 19.7 us -> none  [per_device(): side = lax.all_to_all(sending, lead, 0, 0).reshape(cols * share, -1)]
    all_to_all x1 -> x0, starting transfers between devices: 5.82 us -> none  [per_device(): side = lax.all_to_all(sending, lead, 0, 0).reshape(cols * share, -1)]
  transfers between devices with their start and end apart: 6 -> 5, of which waited for: 4 -> 3; matrix products, arithmetic and copies ran while one was open for 3% -> 3% of each run, Pallas kernels for 0% -> 0%
where the time goes in v4:
time: 110 us
  blocking collectives  59.8 us (54%)
  starting transfers between devices  27.6 us (25%)
  waiting for transfers between devices  12.8 us (12%)
  matrix products  4.73 us (4%)
  local copies, waits for them, and re-layouts  3.17 us (3%)
    all_to_all x1, blocking collectives, per_device(): lax.all_to_all(chip_part.reshape(2 * pairs, -1, chip_part.shape[1]), lead...  27 us
    all_to_all x1, blocking collectives, per_device(): side = lax.all_to_all(sending, lead, 0, 0).reshape(cols * share, -1)  25.8 us
    all_to_all x1, starting transfers between devices, per_device(): lax.all_to_all(out_panels.reshape(2 * cols, share, width), chip_cols, 0, 0)  14.4 us
    all_gather x3, blocking collectives, per_device(): lax.all_gather(weight[at * step:(at + 1) * step], 'core')  7.08 us
    all_to_all x1, starting transfers between devices, per_device(): lax.all_to_all(partial.reshape(2 * cols, share, width), chip_cols, 0, 0)  6.69 us
    ppermute x3, starting transfers between devices, swap(): return lax.ppermute(block, axis, [(0, 1), (1, 0)])  6.46 us
    all_to_all x1, waiting for transfers between devices, per_device(): lax.all_to_all(out_panels.reshape(2 * cols, share, width), chip_cols, 0, 0)  6.41 us
    all_to_all x1, waiting for transfers between devices, per_device(): lax.all_to_all(partial.reshape(2 * cols, share, width), chip_cols, 0, 0)  5.7 us
  transfers between devices with their start and end apart: 5, of which 3 were waited for; matrix products, arithmetic and copies ran while one was open for 3% of the time, Pallas kernels for 0%

profile of v4, /device:TPU:1, one launch (start us, length us, event | category | flops | bytes accessed | tf_op | source)
XLA Modules:
  0.0 109.9 jit_solution(15373925481030230034)
XLA Ops:
  0.6 1.5 %broadcast_in_dim.11 = bf16[2,16,16,384]{3,2,1,0:T(8,128)(2,1)} broadcast(bf16[2,16,384]{2,1,0:T(8,128)(2,1)} %bitcast.44), dimensions={0,2,3} | broadcast | bytes 417792 | tf_op jit(solution)/shard_map/broadcast_in_dim | solution.py:55
  2.2 14.4 %all-to-all-start = ((bf16[32,16,384]{2,1,0:T(8,128)(2,1)}), bf16[32,16,384]{2,1,0:T(8,128)(2,1)S(1)}, u32[]{:S(2)}, u32[]{:S(2)}) async-start(bf16[32,16,384]{2,1,0:T(8,128)(2,1)} %bitcast.2), calls=%async_computation | async-start | bytes 786432 | tf_op jit(solution)/shard_map/all_to_all | solution.py:56
  16.6 1.3 %fusion.18 = (bf16[1,128,1536]{2,1,0:T(8,128)(2,1)S(1)}, bf16[1,128,1536]{2,1,0:T(8,128)(2,1)S(1)}, bf16[1,128,1536]{2,1,0:T(8,128)(2,1)S(1)}) fusion(bf16[1,384,1536]{2,1,0:T(8,128)(2,1)} %param.3), kind=kLoop, calls=%fused_computation.34 | loop fusion | bytes 2359296 | tf_op jit(solution)/shard_map/slice | solution.py:58
  17.9 2.4 %all_gather.12 = bf16[2,128,1536]{2,1,0:T(8,128)(2,1)S(1)} all-gather(bf16[1,128,1536]{2,1,0:T(8,128)(2,1)S(1)} %get-tuple-element.17), channel_id=1, replica_groups=mesh['section'=2,'y'=8,'core'=2,'z'=8,'x_hi'=2] {'core'}, dimensions={0}, use_global_device_ids=true | all-gather | bytes 1179648 | tf_op jit(solution)/shard_map/all_gather | solution.py:58
  20.3 2.4 %all_gather.13 = bf16[2,128,1536]{2,1,0:T(8,128)(2,1)S(1)} all-gather(bf16[1,128,1536]{2,1,0:T(8,128)(2,1)S(1)} %get-tuple-element.18), channel_id=1, replica_groups=mesh['section'=2,'y'=8,'core'=2,'z'=8,'x_hi'=2] {'core'}, dimensions={0}, use_global_device_ids=true | all-gather | bytes 1179648 | tf_op jit(solution)/shard_map/all_gather | solution.py:58
  22.6 2.4 %all_gather.14 = bf16[2,128,1536]{2,1,0:T(8,128)(2,1)S(1)} all-gather(bf16[1,128,1536]{2,1,0:T(8,128)(2,1)S(1)} %get-tuple-element.16), channel_id=1, replica_groups=mesh['section'=2,'y'=8,'core'=2,'z'=8,'x_hi'=2] {'core'}, dimensions={0}, use_global_device_ids=true | all-gather | bytes 1179648 | tf_op jit(solution)/shard_map/all_gather | solution.py:58
  25.0 0.1 constant_dynamic-update-slice_fusion.2
  25.1 0.1 constant_dynamic-update-slice_fusion.1
  25.1 0.1 constant_dynamic-update-slice_fusion
  25.2 6.4 %all-to-all-done = bf16[32,16,384]{2,1,0:T(8,128)(2,1)S(1)} async-done(((bf16[32,16,384]{2,1,0:T(8,128)(2,1)}), bf16[32,16,384]{2,1,0:T(8,128)(2,1)S(1)}, u32[]{:S(2)}, u32[]{:S(2)}) %all-to-all-start) | async-done | bytes 393248 | tf_op jit(solution)/shard_map/all_to_all | solution.py:56
  31.6 0.6 fusion.2
  32.2 0.6 fusion.1
  32.8 27.0 %all_to_all.20 = bf16[16,16,1536]{2,1,0:T(8,128)(2,1)S(1)} all-to-all(bf16[16,16,1536]{2,1,0:T(8,128)(2,1)S(1)} %bitcast.39), channel_id=1, replica_groups=mesh['section'=2,'y'=8,'core'=2,'z'=8,'x_hi'=2] {'section','y'}, dimensions={0} | all-to-all | bytes 1572864 | tf_op jit(solution)/shard_map/all_to_all | solution.py:61
  59.8 0.1 convert_reduce_fusion
  59.8 0.1 slice_reduce_fusion
  59.9 0.1 fusion.15
  60.0 0.1 pad_maximum_fusion
  60.1 25.8 %all_to_all.21 = bf16[16,16,1536]{2,1,0:T(8,128)(2,1)S(1)} all-to-all(bf16[16,16,1536]{2,1,0:T(8,128)(2,1)S(1)} %pad_maximum_fusion), channel_id=1, replica_groups=mesh['section'=2,'y'=8,'core'=2,'z'=8,'x_hi'=2] {'section','y'}, dimensions={0} | all-to-all | bytes 1572864 | tf_op jit(solution)/shard_map/all_to_all | solution.py:67
  85.9 1.6 %convolution_convert_fusion = bf16[2,384,256]{1,2,0:T(8,128)(2,1)} fusion(bf16[2,384,1536]{2,1,0:T(8,128)(2,1)S(1)} %constant_dynamic-update-slice_fusion, bf16[256,1536,1]{1,0,2:T(8,128)(2,1)S(1)} %bitcast.34), kind=kOutput, calls=%fused_computation.4 | convolution fusion | flops 604176384 | bytes 3538944 | tf_op jit(solution)/shard_map/dot_general | solution.py:69
  87.5 6.7 %all-to-all-start.3 = ((bf16[32,16,384]{2,1,0:T(8,128)(2,1)}), bf16[32,16,384]{2,1,0:T(8,128)(2,1)S(1)}, u32[]{:S(2)}, u32[]{:S(2)}) async-start(bf16[32,16,384]{2,1,0:T(8,128)(2,1)} %bitcast.43), calls=%async_computation.3 | async-start | bytes 786432 | tf_op jit(solution)/shard_map/all_to_all | solution.py:70
  94.2 0.1 fusion.19
  94.3 2.1 %collective-permute-start.2 = (bf16[128,1536]{1,0:T(8,128)(2,1)S(1)}, bf16[128,1536]{1,0:T(8,128)(2,1)S(1)}, u32[]{:S(2)}, u32[]{:S(2)}) collective-permute-start(bf16[128,1536]{1,0:T(8,128)(2,1)S(1)} %get-tuple-element.20), channel_id=1, source_target_pairs={{0,16},{16,0},{1,17},{17,1},{2,18},{18,2},{3,19},{19,3},{4,20},{20... | collective-permute-start | bytes 1179656 | tf_op jit(solution)/shard_map/ppermute | solution.py:30
  96.4 2.2 %collective-permute-start.1 = (bf16[128,1536]{1,0:T(8,128)(2,1)S(1)}, bf16[128,1536]{1,0:T(8,128)(2,1)S(1)}, u32[]{:S(2)}, u32[]{:S(2)}) collective-permute-start(bf16[128,1536]{1,0:T(8,128)(2,1)S(1)} %get-tuple-element.19), channel_id=1, source_target_pairs={{0,16},{16,0},{1,17},{17,1},{2,18},{18,2},{3,19},{19,3},{4,20},{20... | collective-permute-start | bytes 1179656 | tf_op jit(solution)/shard_map/ppermute | solution.py:30
  98.6 2.1 %collective-permute-start = (bf16[256,384]{1,0:T(8,128)(2,1)S(1)}, bf16[256,384]{1,0:T(8,128)(2,1)S(1)}, u32[]{:S(2)}, u32[]{:S(2)}) collective-permute-start(bf16[256,384]{1,0:T(8,128)(2,1)S(1)} %dynamic-slice_bitcast_fusion), channel_id=1, source_target_pairs={{0,16},{16,0},{1,17},{17,1},{2,18},{18,2},{3,19},{19,3},{4,20},{20... | collective-permute-start | bytes 589832 | tf_op jit(solution)/shard_map/ppermute | solution.py:30
  100.8 0.5 fusion.6
  101.3 0.7 collective-permute-done
  102.0 0.0 collective-permute-done.2
  102.0 0.0 collective-permute-done.1
  102.0 1.5 %fusion = bf16[384,1536]{1,0:T(8,128)(2,1)} fusion(f32[384,1536]{1,0:T(8,128)S(1)} %fusion.6, bf16[256,384]{1,0:T(8,128)(2,1)S(1)} %collective-permute-done, bf16[128,1536]{1,0:T(8,128)(2,1)S(1)} %collective-permute-done.2, bf16[128,1536]{1,0:T(8,128)(2,1)S(1)} %collective-permute-done.1), kind=kOutput, calls=%fused_computation.1 | convolution fusion | flops 304742400 | bytes 4521984 | tf_op jit(solution)/shard_map/dot_general | solution.py:42
  103.5 5.7 %all-to-all-done.3 = bf16[32,16,384]{2,1,0:T(8,128)(2,1)S(1)} async-done(((bf16[32,16,384]{2,1,0:T(8,128)(2,1)}), bf16[32,16,384]{2,1,0:T(8,128)(2,1)S(1)}, u32[]{:S(2)}, u32[]{:S(2)}) %all-to-all-start.3) | async-done | bytes 393248 | tf_op jit(solution)/shard_map/all_to_all | solution.py:70
  109.2 0.7 bitcast_reduce_fusion
  (4 shorter events, 0.1 us)
Async XLA Ops:
  2.2 29.4 %all-to-all-start = ((bf16[32,16,384]{2,1,0:T(8,128)(2,1)}), bf16[32,16,384]{2,1,0:T(8,128)(2,1)S(1)}, u32[]{:S(2)}, u32[]{:S(2)}) async-start(bf16[32,16,384]{2,1,0:T(8,128)(2,1)} %bitcast.2), calls=%async_computation | async-start | bytes 786432 | tf_op jit(solution)/shard_map/all_to_all | solution.py:56
  87.5 21.7 %all-to-all-start.3 = ((bf16[32,16,384]{2,1,0:T(8,128)(2,1)}), bf16[32,16,384]{2,1,0:T(8,128)(2,1)S(1)}, u32[]{:S(2)}, u32[]{:S(2)}) async-start(bf16[32,16,384]{2,1,0:T(8,128)(2,1)} %bitcast.43), calls=%async_computation.3 | async-start | bytes 786432 | tf_op jit(solution)/shard_map/all_to_all | solution.py:70
  94.3 7.7 %collective-permute-start.2 = (bf16[128,1536]{1,0:T(8,128)(2,1)S(1)}, bf16[128,1536]{1,0:T(8,128)(2,1)S(1)}, u32[]{:S(2)}, u32[]{:S(2)}) collective-permute-start(bf16[128,1536]{1,0:T(8,128)(2,1)S(1)} %get-tuple-element.20), channel_id=1, source_target_pairs={{0,16},{16,0},{1,17},{17,1},{2,18},{18,2},{3,19},{19,3},{4,20},{20... | collective-permute-start | bytes 1179656 | tf_op jit(solution)/shard_map/ppermute | solution.py:30
  96.4 5.6 %collective-permute-start.1 = (bf16[128,1536]{1,0:T(8,128)(2,1)S(1)}, bf16[128,1536]{1,0:T(8,128)(2,1)S(1)}, u32[]{:S(2)}, u32[]{:S(2)}) collective-permute-start(bf16[128,1536]{1,0:T(8,128)(2,1)S(1)} %get-tuple-element.19), channel_id=1, source_target_pairs={{0,16},{16,0},{1,17},{17,1},{2,18},{18,2},{3,19},{19,3},{4,20},{20... | collective-permute-start | bytes 1179656 | tf_op jit(solution)/shard_map/ppermute | solution.py:30
  98.6 3.3 %collective-permute-start = (bf16[256,384]{1,0:T(8,128)(2,1)S(1)}, bf16[256,384]{1,0:T(8,128)(2,1)S(1)}, u32[]{:S(2)}, u32[]{:S(2)}) collective-permute-start(bf16[256,384]{1,0:T(8,128)(2,1)S(1)} %dynamic-slice_bitcast_fusion), channel_id=1, source_target_pairs={{0,16},{16,0},{1,17},{17,1},{2,18},{18,2},{3,19},{19,3},{4,20},{20... | collective-permute-start | bytes 589832 | tf_op jit(solution)/shard_map/ppermute | solution.py:30

commit v5 on v4

--- a/solution.py
+++ b/solution.py
@@ -56,7 +56,7 @@
     gathered = lax.all_to_all(out_panels.reshape(2 * cols, share, width), chip_cols, 0, 0).reshape(2, cols * share, width)
     step = weight.shape[0] // 3
     both = jnp.concatenate([lax.all_gather(weight[at * step : (at + 1) * step], "core") for at in range(3)], axis=1)
-    chip_part = (dot(gathered[0], both[0]) + dot(gathered[1], both[1])).astype(bf16)
+    chip_part = lax.dot_general(gathered, both, (((0, 2), (0, 1)), ((), ())), preferred_element_type=f32).astype(bf16)
 
     blocks = lax.all_to_all(chip_part.reshape(2 * pairs, -1, chip_part.shape[1]), lead, 0, 0)
     preact = blocks[:pairs].astype(f32).sum(0)

time: 110 us -> 110 us (level)
  no operation moved by 1% of the time
where the time goes in v5:
time: 110 us; the launch traced here: 109 us
  blocking collectives  59.8 us (54%)
  starting transfers between devices  27.6 us (25%)
  waiting for transfers between devices  12.8 us (12%)
  matrix products  4.33 us (4%)
  local copies, waits for them, and re-layouts  3.13 us (3%)
    all_to_all x1, blocking collectives, per_device(): lax.all_to_all(chip_part.reshape(2 * pairs, -1, chip_part.shape[1]), lead...  27 us
    all_to_all x1, blocking collectives, per_device(): side = lax.all_to_all(sending, lead, 0, 0).reshape(cols * share, -1)  25.8 us
    all_to_all x1, starting transfers between devices, per_device(): lax.all_to_all(out_panels.reshape(2 * cols, share, width), chip_cols, 0, 0)  14.4 us
    all_gather x3, blocking collectives, per_device(): lax.all_gather(weight[at * step:(at + 1) * step], 'core')  7.08 us
    all_to_all x1, starting transfers between devices, per_device(): lax.all_to_all(partial.reshape(2 * cols, share, width), chip_cols, 0, 0)  6.69 us
    ppermute x3, starting transfers between devices, swap(): return lax.ppermute(block, axis, [(0, 1), (1, 0)])  6.46 us
    all_to_all x1, waiting for transfers between devices, per_device(): lax.all_to_all(out_panels.reshape(2 * cols, share, width), chip_cols, 0, 0)  6.41 us
    all_to_all x1, waiting for transfers between devices, per_device(): lax.all_to_all(partial.reshape(2 * cols, share, width), chip_cols, 0, 0)  5.7 us
  transfers between devices with their start and end apart: 5, of which 3 were waited for; matrix products, arithmetic and copies ran while one was open for 3% of the time, Pallas kernels for 0%

profile of v5, /device:TPU:1, one launch (start us, length us, event | category | flops | bytes accessed | tf_op | source)
XLA Modules:
  0.0 109.4 jit_solution(1568567988320903819)
XLA Ops:
  0.6 1.5 %broadcast_in_dim.11 = bf16[2,16,16,384]{3,2,1,0:T(8,128)(2,1)} broadcast(bf16[2,16,384]{2,1,0:T(8,128)(2,1)} %bitcast.38), dimensions={0,2,3} | broadcast | bytes 417792 | tf_op jit(solution)/shard_map/broadcast_in_dim | solution.py:55
  2.2 14.4 %all-to-all-start = ((bf16[32,16,384]{2,1,0:T(8,128)(2,1)}), bf16[32,16,384]{2,1,0:T(8,128)(2,1)S(1)}, u32[]{:S(2)}, u32[]{:S(2)}) async-start(bf16[32,16,384]{2,1,0:T(8,128)(2,1)} %bitcast.2), calls=%async_computation | async-start | bytes 786432 | tf_op jit(solution)/shard_map/all_to_all | solution.py:56
  16.6 1.3 %fusion.17 = (bf16[1,128,1536]{2,1,0:T(8,128)(2,1)S(1)}, bf16[1,128,1536]{2,1,0:T(8,128)(2,1)S(1)}, bf16[1,128,1536]{2,1,0:T(8,128)(2,1)S(1)}) fusion(bf16[1,384,1536]{2,1,0:T(8,128)(2,1)} %param.3), kind=kLoop, calls=%fused_computation.31 | loop fusion | bytes 2359296 | tf_op jit(solution)/shard_map/slice | solution.py:58
  17.9 2.4 %all_gather.12 = bf16[2,128,1536]{2,1,0:T(8,128)(2,1)S(1)} all-gather(bf16[1,128,1536]{2,1,0:T(8,128)(2,1)S(1)} %get-tuple-element.17), channel_id=1, replica_groups=mesh['section'=2,'y'=8,'core'=2,'z'=8,'x_hi'=2] {'core'}, dimensions={0}, use_global_device_ids=true | all-gather | bytes 1179648 | tf_op jit(solution)/shard_map/all_gather | solution.py:58
  20.3 2.4 %all_gather.13 = bf16[2,128,1536]{2,1,0:T(8,128)(2,1)S(1)} all-gather(bf16[1,128,1536]{2,1,0:T(8,128)(2,1)S(1)} %get-tuple-element.18), channel_id=1, replica_groups=mesh['section'=2,'y'=8,'core'=2,'z'=8,'x_hi'=2] {'core'}, dimensions={0}, use_global_device_ids=true | all-gather | bytes 1179648 | tf_op jit(solution)/shard_map/all_gather | solution.py:58
  22.6 2.4 %all_gather.14 = bf16[2,128,1536]{2,1,0:T(8,128)(2,1)S(1)} all-gather(bf16[1,128,1536]{2,1,0:T(8,128)(2,1)S(1)} %get-tuple-element.16), channel_id=1, replica_groups=mesh['section'=2,'y'=8,'core'=2,'z'=8,'x_hi'=2] {'core'}, dimensions={0}, use_global_device_ids=true | all-gather | bytes 1179648 | tf_op jit(solution)/shard_map/all_gather | solution.py:58
  25.0 0.1 constant_dynamic-update-slice_fusion.2
  25.1 0.1 constant_dynamic-update-slice_fusion.1
  25.1 0.1 constant_dynamic-update-slice_fusion
  25.2 6.4 %all-to-all-done = bf16[32,16,384]{2,1,0:T(8,128)(2,1)S(1)} async-done(((bf16[32,16,384]{2,1,0:T(8,128)(2,1)}), bf16[32,16,384]{2,1,0:T(8,128)(2,1)S(1)}, u32[]{:S(2)}, u32[]{:S(2)}) %all-to-all-start) | async-done | bytes 393248 | tf_op jit(solution)/shard_map/all_to_all | solution.py:56
  31.6 0.8 fusion.1
  32.4 27.0 %all_to_all.20 = bf16[16,16,1536]{2,1,0:T(8,128)(2,1)S(1)} all-to-all(bf16[16,16,1536]{2,1,0:T(8,128)(2,1)S(1)} %bitcast.37), channel_id=1, replica_groups=mesh['section'=2,'y'=8,'core'=2,'z'=8,'x_hi'=2] {'section','y'}, dimensions={0} | all-to-all | bytes 1572864 | tf_op jit(solution)/shard_map/all_to_all | solution.py:61
  59.3 0.1 convert_reduce_fusion
  59.4 0.1 slice_reduce_fusion
  59.5 0.1 fusion.14
  59.6 0.1 pad_maximum_fusion
  59.7 25.8 %all_to_all.21 = bf16[16,16,1536]{2,1,0:T(8,128)(2,1)S(1)} all-to-all(bf16[16,16,1536]{2,1,0:T(8,128)(2,1)S(1)} %pad_maximum_fusion), channel_id=1, replica_groups=mesh['section'=2,'y'=8,'core'=2,'z'=8,'x_hi'=2] {'section','y'}, dimensions={0} | all-to-all | bytes 1572864 | tf_op jit(solution)/shard_map/all_to_all | solution.py:67
  85.5 1.6 %convolution_convert_fusion = bf16[2,384,256]{1,2,0:T(8,128)(2,1)} fusion(bf16[2,384,1536]{2,1,0:T(8,128)(2,1)S(1)} %constant_dynamic-update-slice_fusion, bf16[256,1536,1]{1,0,2:T(8,128)(2,1)S(1)} %bitcast.30), kind=kOutput, calls=%fused_computation.4 | convolution fusion | flops 604176384 | bytes 3538944 | tf_op jit(solution)/shard_map/dot_general | solution.py:69
  87.0 6.7 %all-to-all-start.3 = ((bf16[32,16,384]{2,1,0:T(8,128)(2,1)}), bf16[32,16,384]{2,1,0:T(8,128)(2,1)S(1)}, u32[]{:S(2)}, u32[]{:S(2)}) async-start(bf16[32,16,384]{2,1,0:T(8,128)(2,1)} %bitcast.9), calls=%async_computation.3 | async-start | bytes 786432 | tf_op jit(solution)/shard_map/all_to_all | solution.py:70
  93.7 0.1 fusion.18
  93.8 2.1 %collective-permute-start.2 = (bf16[128,1536]{1,0:T(8,128)(2,1)S(1)}, bf16[128,1536]{1,0:T(8,128)(2,1)S(1)}, u32[]{:S(2)}, u32[]{:S(2)}) collective-permute-start(bf16[128,1536]{1,0:T(8,128)(2,1)S(1)} %get-tuple-element.20), channel_id=1, source_target_pairs={{0,16},{16,0},{1,17},{17,1},{2,18},{18,2},{3,19},{19,3},{4,20},{20... | collective-permute-start | bytes 1179656 | tf_op jit(solution)/shard_map/ppermute | solution.py:30
  95.9 2.2 %collective-permute-start.1 = (bf16[128,1536]{1,0:T(8,128)(2,1)S(1)}, bf16[128,1536]{1,0:T(8,128)(2,1)S(1)}, u32[]{:S(2)}, u32[]{:S(2)}) collective-permute-start(bf16[128,1536]{1,0:T(8,128)(2,1)S(1)} %get-tuple-element.19), channel_id=1, source_target_pairs={{0,16},{16,0},{1,17},{17,1},{2,18},{18,2},{3,19},{19,3},{4,20},{20... | collective-permute-start | bytes 1179656 | tf_op jit(solution)/shard_map/ppermute | solution.py:30
  98.2 2.1 %collective-permute-start = (bf16[256,384]{1,0:T(8,128)(2,1)S(1)}, bf16[256,384]{1,0:T(8,128)(2,1)S(1)}, u32[]{:S(2)}, u32[]{:S(2)}) collective-permute-start(bf16[256,384]{1,0:T(8,128)(2,1)S(1)} %dynamic-slice_bitcast_fusion), channel_id=1, source_target_pairs={{0,16},{16,0},{1,17},{17,1},{2,18},{18,2},{3,19},{19,3},{4,20},{20... | collective-permute-start | bytes 589832 | tf_op jit(solution)/shard_map/ppermute | solution.py:30
  100.3 0.5 fusion.5
  100.8 0.7 collective-permute-done
  101.5 0.0 collective-permute-done.2
  101.5 0.0 collective-permute-done.1
  101.5 1.5 %fusion = bf16[384,1536]{1,0:T(8,128)(2,1)} fusion(f32[384,1536]{1,0:T(8,128)S(1)} %fusion.5, bf16[256,384]{1,0:T(8,128)(2,1)S(1)} %collective-permute-done, bf16[128,1536]{1,0:T(8,128)(2,1)S(1)} %collective-permute-done.2, bf16[128,1536]{1,0:T(8,128)(2,1)S(1)} %collective-permute-done.1), kind=kOutput, calls=%fused_computation.1 | convolution fusion | flops 304742400 | bytes 4521984 | tf_op jit(solution)/shard_map/dot_general | solution.py:42
  103.0 5.7 %all-to-all-done.3 = bf16[32,16,384]{2,1,0:T(8,128)(2,1)S(1)} async-done(((bf16[32,16,384]{2,1,0:T(8,128)(2,1)}), bf16[32,16,384]{2,1,0:T(8,128)(2,1)S(1)}, u32[]{:S(2)}, u32[]{:S(2)}) %all-to-all-start.3) | async-done | bytes 393248 | tf_op jit(solution)/shard_map/all_to_all | solution.py:70
  108.7 0.7 bitcast_reduce_fusion
  (3 shorter events, 0.1 us)
Async XLA Ops:
  2.2 29.4 %all-to-all-start = ((bf16[32,16,384]{2,1,0:T(8,128)(2,1)}), bf16[32,16,384]{2,1,0:T(8,128)(2,1)S(1)}, u32[]{:S(2)}, u32[]{:S(2)}) async-start(bf16[32,16,384]{2,1,0:T(8,128)(2,1)} %bitcast.2), calls=%async_computation | async-start | bytes 786432 | tf_op jit(solution)/shard_map/all_to_all | solution.py:56
  87.0 21.7 %all-to-all-start.3 = ((bf16[32,16,384]{2,1,0:T(8,128)(2,1)}), bf16[32,16,384]{2,1,0:T(8,128)(2,1)S(1)}, u32[]{:S(2)}, u32[]{:S(2)}) async-start(bf16[32,16,384]{2,1,0:T(8,128)(2,1)} %bitcast.9), calls=%async_computation.3 | async-start | bytes 786432 | tf_op jit(solution)/shard_map/all_to_all | solution.py:70
  93.8 7.7 %collective-permute-start.2 = (bf16[128,1536]{1,0:T(8,128)(2,1)S(1)}, bf16[128,1536]{1,0:T(8,128)(2,1)S(1)}, u32[]{:S(2)}, u32[]{:S(2)}) collective-permute-start(bf16[128,1536]{1,0:T(8,128)(2,1)S(1)} %get-tuple-element.20), channel_id=1, source_target_pairs={{0,16},{16,0},{1,17},{17,1},{2,18},{18,2},{3,19},{19,3},{4,20},{20... | collective-permute-start | bytes 1179656 | tf_op jit(solution)/shard_map/ppermute | solution.py:30
  95.9 5.6 %collective-permute-start.1 = (bf16[128,1536]{1,0:T(8,128)(2,1)S(1)}, bf16[128,1536]{1,0:T(8,128)(2,1)S(1)}, u32[]{:S(2)}, u32[]{:S(2)}) collective-permute-start(bf16[128,1536]{1,0:T(8,128)(2,1)S(1)} %get-tuple-element.19), channel_id=1, source_target_pairs={{0,16},{16,0},{1,17},{17,1},{2,18},{18,2},{3,19},{19,3},{4,20},{20... | collective-permute-start | bytes 1179656 | tf_op jit(solution)/shard_map/ppermute | solution.py:30
  98.2 3.3 %collective-permute-start = (bf16[256,384]{1,0:T(8,128)(2,1)S(1)}, bf16[256,384]{1,0:T(8,128)(2,1)S(1)}, u32[]{:S(2)}, u32[]{:S(2)}) collective-permute-start(bf16[256,384]{1,0:T(8,128)(2,1)S(1)} %dynamic-slice_bitcast_fusion), channel_id=1, source_target_pairs={{0,16},{16,0},{1,17},{17,1},{2,18},{18,2},{3,19},{19,3},{4,20},{20... | collective-permute-start | bytes 589832 | tf_op jit(solution)/shard_map/ppermute | solution.py:30

commit v6 on v5

--- a/solution.py
+++ b/solution.py
@@ -42,6 +42,23 @@
     return lax.dot_general(rows, hidden, (((0,), (0,)), ((), ())), preferred_element_type=f32)
 
 
+def over_rows(blocks):
+    chips = lax.axis_size("y")
+    others = 2 * lax.axis_size("z") * lax.axis_size("x_hi")
+    order = [((section + 0) % 2, (at + 4) % chips) for section in range(2) for at in range(chips)]
+    groups = [[(section * chips + chip) * others + at for section, chip in order] for at in range(others)]
+    return lax.all_to_all(blocks, every_axis, 0, 0, axis_index_groups=groups)
+
+
+def over_cols(blocks):
+    deep = lax.axis_size("z")
+    across = deep * 2
+    order = [(core * deep + (at + 5) % deep) * 2 + (side + 1) % 2 for core in range(2) for at in range(deep) for side in range(2)]
+    chips = lax.axis_size("section") * lax.axis_size("y")
+    groups = [[chip * 2 * across + at for at in order] for chip in range(chips)]
+    return lax.all_to_all(blocks, every_axis, 0, 0, axis_index_groups=groups)
+
+
 def per_device(activations, weights):
     panel = activations[0]
     weight = weights[0]
@@ -53,21 +70,21 @@
     width = panel.shape[1]
 
     out_panels = jnp.broadcast_to(panel.reshape(2, 1, share, width), (2, cols, share, width))
-    gathered = lax.all_to_all(out_panels.reshape(2 * cols, share, width), chip_cols, 0, 0).reshape(2, cols * share, width)
+    gathered = over_cols(out_panels.reshape(2 * cols, share, width)).reshape(2, cols * share, width)
     step = weight.shape[0] // 3
     both = jnp.concatenate([lax.all_gather(weight[at * step : (at + 1) * step], "core") for at in range(3)], axis=1)
     chip_part = lax.dot_general(gathered, both, (((0, 2), (0, 1)), ((), ())), preferred_element_type=f32).astype(bf16)
 
-    blocks = lax.all_to_all(chip_part.reshape(2 * pairs, -1, chip_part.shape[1]), lead, 0, 0)
+    blocks = over_rows(chip_part.reshape(2 * pairs, -1, chip_part.shape[1]))
     preact = blocks[:pairs].astype(f32).sum(0)
     dhidden = blocks[pairs:].astype(f32).sum(0).astype(bf16).astype(f32)
     hidden = gelu_value(preact).astype(bf16)
     dpre = (dhidden * gelu_slope(preact)).astype(bf16)
     sending = jnp.concatenate([jnp.broadcast_to(side[None], (pairs, *side.shape)) for side in (dpre, hidden)], axis=0)
-    side = lax.all_to_all(sending, lead, 0, 0).reshape(cols * share, -1)
+    side = over_rows(sending).reshape(cols * share, -1)
 
     partial = lax.dot_general(both, side, (((2,), (1,)), ((), ())), preferred_element_type=f32).astype(bf16).transpose(0, 2, 1)
-    arrived = lax.all_to_all(partial.reshape(2 * cols, share, width), chip_cols, 0, 0)
+    arrived = over_cols(partial.reshape(2 * cols, share, width))
 
     late_gathered, late_side = lax.optimization_barrier((gathered, side))
     late_own = lax.dynamic_slice(late_gathered, (core, jnp.uint32(0), jnp.uint32(0)), (1, *late_gathered.shape[1:]))[0]

time: 110 us -> 105 us (0.955)
  waiting for transfers between devices: 12.8 us -> 2.5 us
  starting transfers between devices: 27.6 us -> 34.5 us
  blocking collectives: 59.8 us -> 58.4 us
    all_to_all x2, waiting for transfers between devices: 12.1 us -> 1.92 us  [over_cols(): return lax.all_to_all(blocks, every_axis, 0, 0, axis_index_groups=groups)]
    all_to_all x2, starting transfers between devices: 21.1 us -> 27.9 us  [over_cols(): return lax.all_to_all(blocks, every_axis, 0, 0, axis_index_groups=groups)]
    all_to_all x2, blocking collectives: 52.8 us -> 51.3 us  [over_rows(): return lax.all_to_all(blocks, every_axis, 0, 0, axis_index_groups=groups)]
where the time goes in v6:
time: 105 us
  blocking collectives  58.4 us (56%)
  starting transfers between devices  34.5 us (33%)
  matrix products  4.33 us (4%)
  local copies, waits for them, and re-layouts  3.13 us (3%)
  waiting for transfers between devices  2.5 us (2%)
    all_to_all x2, blocking collectives, over_rows(): return lax.all_to_all(blocks, every_axis, 0, 0, axis_index_groups=groups)  51.3 us
    all_to_all x2, starting transfers between devices, over_cols(): return lax.all_to_all(blocks, every_axis, 0, 0, axis_index_groups=groups)  27.9 us
    all_gather x3, blocking collectives, per_device(): lax.all_gather(weight[at * step:(at + 1) * step], 'core')  7.08 us
    ppermute x3, starting transfers between devices, swap(): return lax.ppermute(block, axis, [(0, 1), (1, 0)])  6.58 us
  transfers between devices with their start and end apart: 5, of which 3 were waited for; matrix products, arithmetic and copies ran while one was open for 3% of the time, Pallas kernels for 0%

profile of v6, /device:TPU:1, one launch (start us, length us, event | category | flops | bytes accessed | tf_op | source)
XLA Modules:
  0.0 104.5 jit_solution(6414594157380650774)
XLA Ops:
  0.6 1.5 %broadcast_in_dim.11 = bf16[2,16,16,384]{3,2,1,0:T(8,128)(2,1)} broadcast(bf16[2,16,384]{2,1,0:T(8,128)(2,1)} %bitcast.38), dimensions={0,2,3} | broadcast | bytes 417792 | tf_op jit(solution)/shard_map/broadcast_in_dim | solution.py:72
  2.2 16.5 %all-to-all-start = ((bf16[32,16,384]{2,1,0:T(8,128)(2,1)}), bf16[32,16,384]{2,1,0:T(8,128)(2,1)S(1)}, u32[]{:S(2)}, u32[]{:S(2)}) async-start(bf16[32,16,384]{2,1,0:T(8,128)(2,1)} %bitcast.2), calls=%async_computation | async-start | bytes 786432 | tf_op jit(solution)/shard_map/all_to_all | solution.py:59
  18.6 1.3 %fusion.17 = (bf16[1,128,1536]{2,1,0:T(8,128)(2,1)S(1)}, bf16[1,128,1536]{2,1,0:T(8,128)(2,1)S(1)}, bf16[1,128,1536]{2,1,0:T(8,128)(2,1)S(1)}) fusion(bf16[1,384,1536]{2,1,0:T(8,128)(2,1)} %param.3), kind=kLoop, calls=%fused_computation.31 | loop fusion | bytes 2359296 | tf_op jit(solution)/shard_map/slice | solution.py:75
  19.9 2.4 %all_gather.12 = bf16[2,128,1536]{2,1,0:T(8,128)(2,1)S(1)} all-gather(bf16[1,128,1536]{2,1,0:T(8,128)(2,1)S(1)} %get-tuple-element.17), channel_id=1, replica_groups=mesh['section'=2,'y'=8,'core'=2,'z'=8,'x_hi'=2] {'core'}, dimensions={0}, use_global_device_ids=true | all-gather | bytes 1179648 | tf_op jit(solution)/shard_map/all_gather | solution.py:75
  22.3 2.4 %all_gather.13 = bf16[2,128,1536]{2,1,0:T(8,128)(2,1)S(1)} all-gather(bf16[1,128,1536]{2,1,0:T(8,128)(2,1)S(1)} %get-tuple-element.18), channel_id=1, replica_groups=mesh['section'=2,'y'=8,'core'=2,'z'=8,'x_hi'=2] {'core'}, dimensions={0}, use_global_device_ids=true | all-gather | bytes 1179648 | tf_op jit(solution)/shard_map/all_gather | solution.py:75
  24.7 2.4 %all_gather.14 = bf16[2,128,1536]{2,1,0:T(8,128)(2,1)S(1)} all-gather(bf16[1,128,1536]{2,1,0:T(8,128)(2,1)S(1)} %get-tuple-element.16), channel_id=1, replica_groups=mesh['section'=2,'y'=8,'core'=2,'z'=8,'x_hi'=2] {'core'}, dimensions={0}, use_global_device_ids=true | all-gather | bytes 1179648 | tf_op jit(solution)/shard_map/all_gather | solution.py:75
  27.0 0.1 constant_dynamic-update-slice_fusion.2
  27.1 0.1 constant_dynamic-update-slice_fusion.1
  27.1 0.1 constant_dynamic-update-slice_fusion
  27.2 1.3 %all-to-all-done = bf16[32,16,384]{2,1,0:T(8,128)(2,1)S(1)} async-done(((bf16[32,16,384]{2,1,0:T(8,128)(2,1)}), bf16[32,16,384]{2,1,0:T(8,128)(2,1)S(1)}, u32[]{:S(2)}, u32[]{:S(2)}) %all-to-all-start) | async-done | bytes 393248 | tf_op jit(solution)/shard_map/all_to_all | solution.py:59
  28.5 0.8 fusion.1
  29.3 26.0 %all_to_all.20 = bf16[16,16,1536]{2,1,0:T(8,128)(2,1)S(1)} all-to-all(bf16[16,16,1536]{2,1,0:T(8,128)(2,1)S(1)} %bitcast.37), channel_id=1, replica_groups={{128,160,192,224,0,32,64,96,384,416,448,480,256,288,320,352},{129,161,1..., dimensions={0} | all-to-all | bytes 1572864 | tf_op jit(solution)/shard_map/all_to_all | solution.py:50
  55.2 0.1 convert_reduce_fusion
  55.3 0.1 slice_reduce_fusion
  55.4 0.1 fusion.14
  55.5 0.1 pad_maximum_fusion
  55.6 25.3 %all_to_all.21 = bf16[16,16,1536]{2,1,0:T(8,128)(2,1)S(1)} all-to-all(bf16[16,16,1536]{2,1,0:T(8,128)(2,1)S(1)} %pad_maximum_fusion), channel_id=1, replica_groups={{128,160,192,224,0,32,64,96,384,416,448,480,256,288,320,352},{129,161,1..., dimensions={0} | all-to-all | bytes 1572864 | tf_op jit(solution)/shard_map/all_to_all | solution.py:50
  80.9 1.5 %convolution_convert_fusion = bf16[2,384,256]{1,2,0:T(8,128)(2,1)} fusion(bf16[2,384,1536]{2,1,0:T(8,128)(2,1)S(1)} %constant_dynamic-update-slice_fusion, bf16[256,1536,1]{1,0,2:T(8,128)(2,1)S(1)} %bitcast.30), kind=kOutput, calls=%fused_computation.4 | convolution fusion | flops 604176384 | bytes 3538944 | tf_op jit(solution)/shard_map/dot_general | solution.py:86
  82.5 11.5 %all-to-all-start.3 = ((bf16[32,16,384]{2,1,0:T(8,128)(2,1)}), bf16[32,16,384]{2,1,0:T(8,128)(2,1)S(1)}, u32[]{:S(2)}, u32[]{:S(2)}) async-start(bf16[32,16,384]{2,1,0:T(8,128)(2,1)} %bitcast.9), calls=%async_computation.3 | async-start | bytes 786432 | tf_op jit(solution)/shard_map/all_to_all | solution.py:59
  94.0 0.1 fusion.18
  94.0 2.3 %collective-permute-start.2 = (bf16[128,1536]{1,0:T(8,128)(2,1)S(1)}, bf16[128,1536]{1,0:T(8,128)(2,1)S(1)}, u32[]{:S(2)}, u32[]{:S(2)}) collective-permute-start(bf16[128,1536]{1,0:T(8,128)(2,1)S(1)} %get-tuple-element.20), channel_id=1, source_target_pairs={{0,16},{16,0},{1,17},{17,1},{2,18},{18,2},{3,19},{19,3},{4,20},{20... | collective-permute-start | bytes 1179656 | tf_op jit(solution)/shard_map/ppermute | solution.py:30
  96.3 2.1 %collective-permute-start.1 = (bf16[128,1536]{1,0:T(8,128)(2,1)S(1)}, bf16[128,1536]{1,0:T(8,128)(2,1)S(1)}, u32[]{:S(2)}, u32[]{:S(2)}) collective-permute-start(bf16[128,1536]{1,0:T(8,128)(2,1)S(1)} %get-tuple-element.19), channel_id=1, source_target_pairs={{0,16},{16,0},{1,17},{17,1},{2,18},{18,2},{3,19},{19,3},{4,20},{20... | collective-permute-start | bytes 1179656 | tf_op jit(solution)/shard_map/ppermute | solution.py:30
  98.4 2.3 %collective-permute-start = (bf16[256,384]{1,0:T(8,128)(2,1)S(1)}, bf16[256,384]{1,0:T(8,128)(2,1)S(1)}, u32[]{:S(2)}, u32[]{:S(2)}) collective-permute-start(bf16[256,384]{1,0:T(8,128)(2,1)S(1)} %dynamic-slice_bitcast_fusion), channel_id=1, source_target_pairs={{0,16},{16,0},{1,17},{17,1},{2,18},{18,2},{3,19},{19,3},{4,20},{20... | collective-permute-start | bytes 589832 | tf_op jit(solution)/shard_map/ppermute | solution.py:30
  100.7 0.5 fusion.5
  101.2 0.6 collective-permute-done
  101.7 0.0 collective-permute-done.2
  101.7 0.0 collective-permute-done.1
  101.8 1.5 %fusion = bf16[384,1536]{1,0:T(8,128)(2,1)} fusion(f32[384,1536]{1,0:T(8,128)S(1)} %fusion.5, bf16[256,384]{1,0:T(8,128)(2,1)S(1)} %collective-permute-done, bf16[128,1536]{1,0:T(8,128)(2,1)S(1)} %collective-permute-done.2, bf16[128,1536]{1,0:T(8,128)(2,1)S(1)} %collective-permute-done.1), kind=kOutput, calls=%fused_computation.1 | convolution fusion | flops 304742400 | bytes 4521984 | tf_op jit(solution)/shard_map/dot_general | solution.py:42
  103.3 0.6 all-to-all-done.3
  103.9 0.7 bitcast_reduce_fusion
  (3 shorter events, 0.1 us)
Async XLA Ops:
  2.2 26.4 %all-to-all-start = ((bf16[32,16,384]{2,1,0:T(8,128)(2,1)}), bf16[32,16,384]{2,1,0:T(8,128)(2,1)S(1)}, u32[]{:S(2)}, u32[]{:S(2)}) async-start(bf16[32,16,384]{2,1,0:T(8,128)(2,1)} %bitcast.2), calls=%async_computation | async-start | bytes 786432 | tf_op jit(solution)/shard_map/all_to_all | solution.py:59
  82.5 21.4 %all-to-all-start.3 = ((bf16[32,16,384]{2,1,0:T(8,128)(2,1)}), bf16[32,16,384]{2,1,0:T(8,128)(2,1)S(1)}, u32[]{:S(2)}, u32[]{:S(2)}) async-start(bf16[32,16,384]{2,1,0:T(8,128)(2,1)} %bitcast.9), calls=%async_computation.3 | async-start | bytes 786432 | tf_op jit(solution)/shard_map/all_to_all | solution.py:59
  94.0 7.7 %collective-permute-start.2 = (bf16[128,1536]{1,0:T(8,128)(2,1)S(1)}, bf16[128,1536]{1,0:T(8,128)(2,1)S(1)}, u32[]{:S(2)}, u32[]{:S(2)}) collective-permute-start(bf16[128,1536]{1,0:T(8,128)(2,1)S(1)} %get-tuple-element.20), channel_id=1, source_target_pairs={{0,16},{16,0},{1,17},{17,1},{2,18},{18,2},{3,19},{19,3},{4,20},{20... | collective-permute-start | bytes 1179656 | tf_op jit(solution)/shard_map/ppermute | solution.py:30
  96.3 5.5 %collective-permute-start.1 = (bf16[128,1536]{1,0:T(8,128)(2,1)S(1)}, bf16[128,1536]{1,0:T(8,128)(2,1)S(1)}, u32[]{:S(2)}, u32[]{:S(2)}) collective-permute-start(bf16[128,1536]{1,0:T(8,128)(2,1)S(1)} %get-tuple-element.19), channel_id=1, source_target_pairs={{0,16},{16,0},{1,17},{17,1},{2,18},{18,2},{3,19},{19,3},{4,20},{20... | collective-permute-start | bytes 1179656 | tf_op jit(solution)/shard_map/ppermute | solution.py:30
  98.4 3.3 %collective-permute-start = (bf16[256,384]{1,0:T(8,128)(2,1)S(1)}, bf16[256,384]{1,0:T(8,128)(2,1)S(1)}, u32[]{:S(2)}, u32[]{:S(2)}) collective-permute-start(bf16[256,384]{1,0:T(8,128)(2,1)S(1)} %dynamic-slice_bitcast_fusion), channel_id=1, source_target_pairs={{0,16},{16,0},{1,17},{17,1},{2,18},{18,2},{3,19},{19,3},{4,20},{20... | collective-permute-start | bytes 589832 | tf_op jit(solution)/shard_map/ppermute | solution.py:30

commit v7 on v6

--- a/solution.py
+++ b/solution.py
@@ -45,7 +45,7 @@
 def over_rows(blocks):
     chips = lax.axis_size("y")
     others = 2 * lax.axis_size("z") * lax.axis_size("x_hi")
-    order = [((section + 0) % 2, (at + 4) % chips) for section in range(2) for at in range(chips)]
+    order = [(section, (4 + (at // 2 if at % 2 == 0 else -(at + 1) // 2)) % chips) for section in range(2) for at in range(chips)]
     groups = [[(section * chips + chip) * others + at for section, chip in order] for at in range(others)]
     return lax.all_to_all(blocks, every_axis, 0, 0, axis_index_groups=groups)
 

time: 105 us -> 105 us (level)
  blocking collectives: 58.4 us -> 56.3 us
  starting transfers between devices: 34.5 us -> 36.2 us
    all_to_all x2, blocking collectives: 51.3 us -> 49.2 us  [over_rows(): return lax.all_to_all(blocks, every_axis, 0, 0, axis_index_groups=groups)]
    all_to_all x2, starting transfers between devices: 27.9 us -> 29.6 us  [over_cols(): return lax.all_to_all(blocks, every_axis, 0, 0, axis_index_groups=groups)]
where the time goes in v7:
time: 105 us; the launch traced here: 104 us
  blocking collectives  56.3 us (54%)
  starting transfers between devices  36.2 us (34%)
  matrix products  4.32 us (4%)
  local copies, waits for them, and re-layouts  3.13 us (3%)
  waiting for transfers between devices  2.5 us (2%)
    all_to_all x2, blocking collectives, over_rows(): return lax.all_to_all(blocks, every_axis, 0, 0, axis_index_groups=groups)  49.2 us
    all_to_all x2, starting transfers between devices, over_cols(): return lax.all_to_all(blocks, every_axis, 0, 0, axis_index_groups=groups)  29.6 us
    all_gather x3, blocking collectives, per_device(): lax.all_gather(weight[at * step:(at + 1) * step], 'core')  7.08 us
    ppermute x3, starting transfers between devices, swap(): return lax.ppermute(block, axis, [(0, 1), (1, 0)])  6.58 us
  transfers between devices with their start and end apart: 5, of which 3 were waited for; matrix products, arithmetic and copies ran while one was open for 3% of the time, Pallas kernels for 0%

profile of v7, /device:TPU:1, one launch (start us, length us, event | category | flops | bytes accessed | tf_op | source)
XLA Modules:
  0.0 104.1 jit_solution(10477775361787140822)
XLA Ops:
  0.6 1.5 %broadcast_in_dim.11 = bf16[2,16,16,384]{3,2,1,0:T(8,128)(2,1)} broadcast(bf16[2,16,384]{2,1,0:T(8,128)(2,1)} %bitcast.38), dimensions={0,2,3} | broadcast | bytes 417792 | tf_op jit(solution)/shard_map/broadcast_in_dim | solution.py:72
  2.2 16.5 %all-to-all-start = ((bf16[32,16,384]{2,1,0:T(8,128)(2,1)}), bf16[32,16,384]{2,1,0:T(8,128)(2,1)S(1)}, u32[]{:S(2)}, u32[]{:S(2)}) async-start(bf16[32,16,384]{2,1,0:T(8,128)(2,1)} %bitcast.2), calls=%async_computation | async-start | bytes 786432 | tf_op jit(solution)/shard_map/all_to_all | solution.py:59
  18.6 1.3 %fusion.17 = (bf16[1,128,1536]{2,1,0:T(8,128)(2,1)S(1)}, bf16[1,128,1536]{2,1,0:T(8,128)(2,1)S(1)}, bf16[1,128,1536]{2,1,0:T(8,128)(2,1)S(1)}) fusion(bf16[1,384,1536]{2,1,0:T(8,128)(2,1)} %param.3), kind=kLoop, calls=%fused_computation.31 | loop fusion | bytes 2359296 | tf_op jit(solution)/shard_map/slice | solution.py:75
  19.9 2.4 %all_gather.12 = bf16[2,128,1536]{2,1,0:T(8,128)(2,1)S(1)} all-gather(bf16[1,128,1536]{2,1,0:T(8,128)(2,1)S(1)} %get-tuple-element.17), channel_id=1, replica_groups=mesh['section'=2,'y'=8,'core'=2,'z'=8,'x_hi'=2] {'core'}, dimensions={0}, use_global_device_ids=true | all-gather | bytes 1179648 | tf_op jit(solution)/shard_map/all_gather | solution.py:75
  22.3 2.4 %all_gather.13 = bf16[2,128,1536]{2,1,0:T(8,128)(2,1)S(1)} all-gather(bf16[1,128,1536]{2,1,0:T(8,128)(2,1)S(1)} %get-tuple-element.18), channel_id=1, replica_groups=mesh['section'=2,'y'=8,'core'=2,'z'=8,'x_hi'=2] {'core'}, dimensions={0}, use_global_device_ids=true | all-gather | bytes 1179648 | tf_op jit(solution)/shard_map/all_gather | solution.py:75
  24.7 2.4 %all_gather.14 = bf16[2,128,1536]{2,1,0:T(8,128)(2,1)S(1)} all-gather(bf16[1,128,1536]{2,1,0:T(8,128)(2,1)S(1)} %get-tuple-element.16), channel_id=1, replica_groups=mesh['section'=2,'y'=8,'core'=2,'z'=8,'x_hi'=2] {'core'}, dimensions={0}, use_global_device_ids=true | all-gather | bytes 1179648 | tf_op jit(solution)/shard_map/all_gather | solution.py:75
  27.0 0.1 constant_dynamic-update-slice_fusion.2
  27.1 0.1 constant_dynamic-update-slice_fusion.1
  27.1 0.1 constant_dynamic-update-slice_fusion
  27.2 1.3 %all-to-all-done = bf16[32,16,384]{2,1,0:T(8,128)(2,1)S(1)} async-done(((bf16[32,16,384]{2,1,0:T(8,128)(2,1)}), bf16[32,16,384]{2,1,0:T(8,128)(2,1)S(1)}, u32[]{:S(2)}, u32[]{:S(2)}) %all-to-all-start) | async-done | bytes 393248 | tf_op jit(solution)/shard_map/all_to_all | solution.py:59
  28.5 0.8 fusion.1
  29.3 26.0 %all_to_all.20 = bf16[16,16,1536]{2,1,0:T(8,128)(2,1)S(1)} all-to-all(bf16[16,16,1536]{2,1,0:T(8,128)(2,1)S(1)} %bitcast.37), channel_id=1, replica_groups={{128,96,160,64,192,32,224,0,384,352,416,320,448,288,480,256},{129,97,16..., dimensions={0} | all-to-all | bytes 1572864 | tf_op jit(solution)/shard_map/all_to_all | solution.py:50
  55.3 0.1 convert_reduce_fusion
  55.4 0.1 slice_reduce_fusion
  55.4 0.1 fusion.14
  55.6 0.1 pad_maximum_fusion
  55.7 23.2 %all_to_all.21 = bf16[16,16,1536]{2,1,0:T(8,128)(2,1)S(1)} all-to-all(bf16[16,16,1536]{2,1,0:T(8,128)(2,1)S(1)} %pad_maximum_fusion), channel_id=1, replica_groups={{128,96,160,64,192,32,224,0,384,352,416,320,448,288,480,256},{129,97,16..., dimensions={0} | all-to-all | bytes 1572864 | tf_op jit(solution)/shard_map/all_to_all | solution.py:50
  78.8 1.5 %convolution_convert_fusion = bf16[2,384,256]{1,2,0:T(8,128)(2,1)} fusion(bf16[2,384,1536]{2,1,0:T(8,128)(2,1)S(1)} %constant_dynamic-update-slice_fusion, bf16[256,1536,1]{1,0,2:T(8,128)(2,1)S(1)} %bitcast.30), kind=kOutput, calls=%fused_computation.4 | convolution fusion | flops 604176384 | bytes 3538944 | tf_op jit(solution)/shard_map/dot_general | solution.py:86
  80.4 13.2 %all-to-all-start.3 = ((bf16[32,16,384]{2,1,0:T(8,128)(2,1)}), bf16[32,16,384]{2,1,0:T(8,128)(2,1)S(1)}, u32[]{:S(2)}, u32[]{:S(2)}) async-start(bf16[32,16,384]{2,1,0:T(8,128)(2,1)} %bitcast.9), calls=%async_computation.3 | async-start | bytes 786432 | tf_op jit(solution)/shard_map/all_to_all | solution.py:59
  93.6 0.1 fusion.18
  93.6 2.3 %collective-permute-start.2 = (bf16[128,1536]{1,0:T(8,128)(2,1)S(1)}, bf16[128,1536]{1,0:T(8,128)(2,1)S(1)}, u32[]{:S(2)}, u32[]{:S(2)}) collective-permute-start(bf16[128,1536]{1,0:T(8,128)(2,1)S(1)} %get-tuple-element.20), channel_id=1, source_target_pairs={{0,16},{16,0},{1,17},{17,1},{2,18},{18,2},{3,19},{19,3},{4,20},{20... | collective-permute-start | bytes 1179656 | tf_op jit(solution)/shard_map/ppermute | solution.py:30
  95.9 2.1 %collective-permute-start.1 = (bf16[128,1536]{1,0:T(8,128)(2,1)S(1)}, bf16[128,1536]{1,0:T(8,128)(2,1)S(1)}, u32[]{:S(2)}, u32[]{:S(2)}) collective-permute-start(bf16[128,1536]{1,0:T(8,128)(2,1)S(1)} %get-tuple-element.19), channel_id=1, source_target_pairs={{0,16},{16,0},{1,17},{17,1},{2,18},{18,2},{3,19},{19,3},{4,20},{20... | collective-permute-start | bytes 1179656 | tf_op jit(solution)/shard_map/ppermute | solution.py:30
  98.0 2.3 %collective-permute-start = (bf16[256,384]{1,0:T(8,128)(2,1)S(1)}, bf16[256,384]{1,0:T(8,128)(2,1)S(1)}, u32[]{:S(2)}, u32[]{:S(2)}) collective-permute-start(bf16[256,384]{1,0:T(8,128)(2,1)S(1)} %dynamic-slice_bitcast_fusion), channel_id=1, source_target_pairs={{0,16},{16,0},{1,17},{17,1},{2,18},{18,2},{3,19},{19,3},{4,20},{20... | collective-permute-start | bytes 589832 | tf_op jit(solution)/shard_map/ppermute | solution.py:30
  100.3 0.5 fusion.5
  100.8 0.6 collective-permute-done
  101.4 0.0 collective-permute-done.2
  101.4 0.0 collective-permute-done.1
  101.4 1.5 %fusion = bf16[384,1536]{1,0:T(8,128)(2,1)} fusion(f32[384,1536]{1,0:T(8,128)S(1)} %fusion.5, bf16[256,384]{1,0:T(8,128)(2,1)S(1)} %collective-permute-done, bf16[128,1536]{1,0:T(8,128)(2,1)S(1)} %collective-permute-done.2, bf16[128,1536]{1,0:T(8,128)(2,1)S(1)} %collective-permute-done.1), kind=kOutput, calls=%fused_computation.1 | convolution fusion | flops 304742400 | bytes 4521984 | tf_op jit(solution)/shard_map/dot_general | solution.py:42
  102.9 0.6 all-to-all-done.3
  103.5 0.7 bitcast_reduce_fusion
  (3 shorter events, 0.1 us)
Async XLA Ops:
  2.2 26.4 %all-to-all-start = ((bf16[32,16,384]{2,1,0:T(8,128)(2,1)}), bf16[32,16,384]{2,1,0:T(8,128)(2,1)S(1)}, u32[]{:S(2)}, u32[]{:S(2)}) async-start(bf16[32,16,384]{2,1,0:T(8,128)(2,1)} %bitcast.2), calls=%async_computation | async-start | bytes 786432 | tf_op jit(solution)/shard_map/all_to_all | solution.py:59
  80.4 23.1 %all-to-all-start.3 = ((bf16[32,16,384]{2,1,0:T(8,128)(2,1)}), bf16[32,16,384]{2,1,0:T(8,128)(2,1)S(1)}, u32[]{:S(2)}, u32[]{:S(2)}) async-start(bf16[32,16,384]{2,1,0:T(8,128)(2,1)} %bitcast.9), calls=%async_computation.3 | async-start | bytes 786432 | tf_op jit(solution)/shard_map/all_to_all | solution.py:59
  93.6 7.7 %collective-permute-start.2 = (bf16[128,1536]{1,0:T(8,128)(2,1)S(1)}, bf16[128,1536]{1,0:T(8,128)(2,1)S(1)}, u32[]{:S(2)}, u32[]{:S(2)}) collective-permute-start(bf16[128,1536]{1,0:T(8,128)(2,1)S(1)} %get-tuple-element.20), channel_id=1, source_target_pairs={{0,16},{16,0},{1,17},{17,1},{2,18},{18,2},{3,19},{19,3},{4,20},{20... | collective-permute-start | bytes 1179656 | tf_op jit(solution)/shard_map/ppermute | solution.py:30
  95.9 5.5 %collective-permute-start.1 = (bf16[128,1536]{1,0:T(8,128)(2,1)S(1)}, bf16[128,1536]{1,0:T(8,128)(2,1)S(1)}, u32[]{:S(2)}, u32[]{:S(2)}) collective-permute-start(bf16[128,1536]{1,0:T(8,128)(2,1)S(1)} %get-tuple-element.19), channel_id=1, source_target_pairs={{0,16},{16,0},{1,17},{17,1},{2,18},{18,2},{3,19},{19,3},{4,20},{20... | collective-permute-start | bytes 1179656 | tf_op jit(solution)/shard_map/ppermute | solution.py:30
  98.0 3.3 %collective-permute-start = (bf16[256,384]{1,0:T(8,128)(2,1)S(1)}, bf16[256,384]{1,0:T(8,128)(2,1)S(1)}, u32[]{:S(2)}, u32[]{:S(2)}) collective-permute-start(bf16[256,384]{1,0:T(8,128)(2,1)S(1)} %dynamic-slice_bitcast_fusion), channel_id=1, source_target_pairs={{0,16},{16,0},{1,17},{17,1},{2,18},{18,2},{3,19},{19,3},{4,20},{20... | collective-permute-start | bytes 589832 | tf_op jit(solution)/shard_map/ppermute | solution.py:30

commit v8 on v7

--- a/solution.py
+++ b/solution.py
@@ -45,8 +45,12 @@
 def over_rows(blocks):
     chips = lax.axis_size("y")
     others = 2 * lax.axis_size("z") * lax.axis_size("x_hi")
-    order = [(section, (4 + (at // 2 if at % 2 == 0 else -(at + 1) // 2)) % chips) for section in range(2) for at in range(chips)]
-    groups = [[(section * chips + chip) * others + at for section, chip in order] for at in range(others)]
+    groups = []
+    for at in range(others):
+        first = (6, 4)[at // (others // 2)]
+        groups.append(
+            [(section * chips + (turn + first) % chips) * others + at for section in range(2) for turn in range(chips)]
+        )
     return lax.all_to_all(blocks, every_axis, 0, 0, axis_index_groups=groups)
 
 

time: 105 us -> 105 us (level)
  blocking collectives: 56.3 us -> 58.5 us
  starting transfers between devices: 36.2 us -> 34.1 us
    all_to_all x2, blocking collectives: 49.2 us -> 51.5 us  [over_rows(): return lax.all_to_all(blocks, every_axis, 0, 0, axis_index_groups=groups)]
    all_to_all x2, starting transfers between devices: 29.6 us -> 27.6 us  [over_cols(): return lax.all_to_all(blocks, every_axis, 0, 0, axis_index_groups=groups)]
where the time goes in v8:
time: 105 us; the launch traced here: 104 us
  blocking collectives  58.5 us (56%)
  starting transfers between devices  34.1 us (32%)
  matrix products  4.32 us (4%)
  local copies, waits for them, and re-layouts  3.13 us (3%)
  waiting for transfers between devices  2.5 us (2%)
    all_to_all x2, blocking collectives, over_rows(): return lax.all_to_all(blocks, every_axis, 0, 0, axis_index_groups=groups)  51.5 us
    all_to_all x2, starting transfers between devices, over_cols(): return lax.all_to_all(blocks, every_axis, 0, 0, axis_index_groups=groups)  27.6 us
    all_gather x3, blocking collectives, per_device(): lax.all_gather(weight[at * step:(at + 1) * step], 'core')  7.08 us
    ppermute x3, starting transfers between devices, swap(): return lax.ppermute(block, axis, [(0, 1), (1, 0)])  6.58 us
  transfers between devices with their start and end apart: 5, of which 3 were waited for; matrix products, arithmetic and copies ran while one was open for 3% of the time, Pallas kernels for 0%

profile of v8, /device:TPU:1, one launch (start us, length us, event | category | flops | bytes accessed | tf_op | source)
XLA Modules:
  0.0 104.3 jit_solution(3106219681625330057)
XLA Ops:
  0.6 1.5 %broadcast_in_dim.11 = bf16[2,16,16,384]{3,2,1,0:T(8,128)(2,1)} broadcast(bf16[2,16,384]{2,1,0:T(8,128)(2,1)} %bitcast.38), dimensions={0,2,3} | broadcast | bytes 417792 | tf_op jit(solution)/shard_map/broadcast_in_dim | solution.py:76
  2.2 16.5 %all-to-all-start = ((bf16[32,16,384]{2,1,0:T(8,128)(2,1)}), bf16[32,16,384]{2,1,0:T(8,128)(2,1)S(1)}, u32[]{:S(2)}, u32[]{:S(2)}) async-start(bf16[32,16,384]{2,1,0:T(8,128)(2,1)} %bitcast.2), calls=%async_computation | async-start | bytes 786432 | tf_op jit(solution)/shard_map/all_to_all | solution.py:63
  18.6 1.3 %fusion.17 = (bf16[1,128,1536]{2,1,0:T(8,128)(2,1)S(1)}, bf16[1,128,1536]{2,1,0:T(8,128)(2,1)S(1)}, bf16[1,128,1536]{2,1,0:T(8,128)(2,1)S(1)}) fusion(bf16[1,384,1536]{2,1,0:T(8,128)(2,1)} %param.3), kind=kLoop, calls=%fused_computation.31 | loop fusion | bytes 2359296 | tf_op jit(solution)/shard_map/slice | solution.py:79
  19.9 2.4 %all_gather.12 = bf16[2,128,1536]{2,1,0:T(8,128)(2,1)S(1)} all-gather(bf16[1,128,1536]{2,1,0:T(8,128)(2,1)S(1)} %get-tuple-element.17), channel_id=1, replica_groups=mesh['section'=2,'y'=8,'core'=2,'z'=8,'x_hi'=2] {'core'}, dimensions={0}, use_global_device_ids=true | all-gather | bytes 1179648 | tf_op jit(solution)/shard_map/all_gather | solution.py:79
  22.3 2.4 %all_gather.13 = bf16[2,128,1536]{2,1,0:T(8,128)(2,1)S(1)} all-gather(bf16[1,128,1536]{2,1,0:T(8,128)(2,1)S(1)} %get-tuple-element.18), channel_id=1, replica_groups=mesh['section'=2,'y'=8,'core'=2,'z'=8,'x_hi'=2] {'core'}, dimensions={0}, use_global_device_ids=true | all-gather | bytes 1179648 | tf_op jit(solution)/shard_map/all_gather | solution.py:79
  24.7 2.4 %all_gather.14 = bf16[2,128,1536]{2,1,0:T(8,128)(2,1)S(1)} all-gather(bf16[1,128,1536]{2,1,0:T(8,128)(2,1)S(1)} %get-tuple-element.16), channel_id=1, replica_groups=mesh['section'=2,'y'=8,'core'=2,'z'=8,'x_hi'=2] {'core'}, dimensions={0}, use_global_device_ids=true | all-gather | bytes 1179648 | tf_op jit(solution)/shard_map/all_gather | solution.py:79
  27.0 0.1 constant_dynamic-update-slice_fusion.2
  27.1 0.1 constant_dynamic-update-slice_fusion.1
  27.1 0.1 constant_dynamic-update-slice_fusion
  27.2 1.3 %all-to-all-done = bf16[32,16,384]{2,1,0:T(8,128)(2,1)S(1)} async-done(((bf16[32,16,384]{2,1,0:T(8,128)(2,1)}), bf16[32,16,384]{2,1,0:T(8,128)(2,1)S(1)}, u32[]{:S(2)}, u32[]{:S(2)}) %all-to-all-start) | async-done | bytes 393248 | tf_op jit(solution)/shard_map/all_to_all | solution.py:63
  28.5 0.8 fusion.1
  29.3 26.1 %all_to_all.20 = bf16[16,16,1536]{2,1,0:T(8,128)(2,1)S(1)} all-to-all(bf16[16,16,1536]{2,1,0:T(8,128)(2,1)S(1)} %bitcast.37), channel_id=1, replica_groups={{192,224,0,32,64,96,128,160,448,480,256,288,320,352,384,416},{193,225,1..., dimensions={0} | all-to-all | bytes 1572864 | tf_op jit(solution)/shard_map/all_to_all | solution.py:54
  55.4 0.1 convert_reduce_fusion
  55.5 0.1 slice_reduce_fusion
  55.5 0.1 fusion.14
  55.7 0.1 pad_maximum_fusion
  55.8 25.3 %all_to_all.21 = bf16[16,16,1536]{2,1,0:T(8,128)(2,1)S(1)} all-to-all(bf16[16,16,1536]{2,1,0:T(8,128)(2,1)S(1)} %pad_maximum_fusion), channel_id=1, replica_groups={{192,224,0,32,64,96,128,160,448,480,256,288,320,352,384,416},{193,225,1..., dimensions={0} | all-to-all | bytes 1572864 | tf_op jit(solution)/shard_map/all_to_all | solution.py:54
  81.1 1.5 %convolution_convert_fusion = bf16[2,384,256]{1,2,0:T(8,128)(2,1)} fusion(bf16[2,384,1536]{2,1,0:T(8,128)(2,1)S(1)} %constant_dynamic-update-slice_fusion, bf16[256,1536,1]{1,0,2:T(8,128)(2,1)S(1)} %bitcast.30), kind=kOutput, calls=%fused_computation.4 | convolution fusion | flops 604176384 | bytes 3538944 | tf_op jit(solution)/shard_map/dot_general | solution.py:90
  82.6 11.1 %all-to-all-start.3 = ((bf16[32,16,384]{2,1,0:T(8,128)(2,1)}), bf16[32,16,384]{2,1,0:T(8,128)(2,1)S(1)}, u32[]{:S(2)}, u32[]{:S(2)}) async-start(bf16[32,16,384]{2,1,0:T(8,128)(2,1)} %bitcast.9), calls=%async_computation.3 | async-start | bytes 786432 | tf_op jit(solution)/shard_map/all_to_all | solution.py:63
  93.7 0.1 fusion.18
  93.8 2.3 %collective-permute-start.2 = (bf16[128,1536]{1,0:T(8,128)(2,1)S(1)}, bf16[128,1536]{1,0:T(8,128)(2,1)S(1)}, u32[]{:S(2)}, u32[]{:S(2)}) collective-permute-start(bf16[128,1536]{1,0:T(8,128)(2,1)S(1)} %get-tuple-element.20), channel_id=1, source_target_pairs={{0,16},{16,0},{1,17},{17,1},{2,18},{18,2},{3,19},{19,3},{4,20},{20... | collective-permute-start | bytes 1179656 | tf_op jit(solution)/shard_map/ppermute | solution.py:30
  96.1 2.1 %collective-permute-start.1 = (bf16[128,1536]{1,0:T(8,128)(2,1)S(1)}, bf16[128,1536]{1,0:T(8,128)(2,1)S(1)}, u32[]{:S(2)}, u32[]{:S(2)}) collective-permute-start(bf16[128,1536]{1,0:T(8,128)(2,1)S(1)} %get-tuple-element.19), channel_id=1, source_target_pairs={{0,16},{16,0},{1,17},{17,1},{2,18},{18,2},{3,19},{19,3},{4,20},{20... | collective-permute-start | bytes 1179656 | tf_op jit(solution)/shard_map/ppermute | solution.py:30
  98.2 2.3 %collective-permute-start = (bf16[256,384]{1,0:T(8,128)(2,1)S(1)}, bf16[256,384]{1,0:T(8,128)(2,1)S(1)}, u32[]{:S(2)}, u32[]{:S(2)}) collective-permute-start(bf16[256,384]{1,0:T(8,128)(2,1)S(1)} %dynamic-slice_bitcast_fusion), channel_id=1, source_target_pairs={{0,16},{16,0},{1,17},{17,1},{2,18},{18,2},{3,19},{19,3},{4,20},{20... | collective-permute-start | bytes 589832 | tf_op jit(solution)/shard_map/ppermute | solution.py:30
  100.5 0.5 fusion.5
  101.0 0.6 collective-permute-done
  101.5 0.0 collective-permute-done.2
  101.5 0.0 collective-permute-done.1
  101.5 1.5 %fusion = bf16[384,1536]{1,0:T(8,128)(2,1)} fusion(f32[384,1536]{1,0:T(8,128)S(1)} %fusion.5, bf16[256,384]{1,0:T(8,128)(2,1)S(1)} %collective-permute-done, bf16[128,1536]{1,0:T(8,128)(2,1)S(1)} %collective-permute-done.2, bf16[128,1536]{1,0:T(8,128)(2,1)S(1)} %collective-permute-done.1), kind=kOutput, calls=%fused_computation.1 | convolution fusion | flops 304742400 | bytes 4521984 | tf_op jit(solution)/shard_map/dot_general | solution.py:42
  103.0 0.6 all-to-all-done.3
  103.6 0.7 bitcast_reduce_fusion
  (3 shorter events, 0.1 us)
Async XLA Ops:
  2.2 26.4 %all-to-all-start = ((bf16[32,16,384]{2,1,0:T(8,128)(2,1)}), bf16[32,16,384]{2,1,0:T(8,128)(2,1)S(1)}, u32[]{:S(2)}, u32[]{:S(2)}) async-start(bf16[32,16,384]{2,1,0:T(8,128)(2,1)} %bitcast.2), calls=%async_computation | async-start | bytes 786432 | tf_op jit(solution)/shard_map/all_to_all | solution.py:63
  82.6 21.0 %all-to-all-start.3 = ((bf16[32,16,384]{2,1,0:T(8,128)(2,1)}), bf16[32,16,384]{2,1,0:T(8,128)(2,1)S(1)}, u32[]{:S(2)}, u32[]{:S(2)}) async-start(bf16[32,16,384]{2,1,0:T(8,128)(2,1)} %bitcast.9), calls=%async_computation.3 | async-start | bytes 786432 | tf_op jit(solution)/shard_map/all_to_all | solution.py:63
  93.8 7.7 %collective-permute-start.2 = (bf16[128,1536]{1,0:T(8,128)(2,1)S(1)}, bf16[128,1536]{1,0:T(8,128)(2,1)S(1)}, u32[]{:S(2)}, u32[]{:S(2)}) collective-permute-start(bf16[128,1536]{1,0:T(8,128)(2,1)S(1)} %get-tuple-element.20), channel_id=1, source_target_pairs={{0,16},{16,0},{1,17},{17,1},{2,18},{18,2},{3,19},{19,3},{4,20},{20... | collective-permute-start | bytes 1179656 | tf_op jit(solution)/shard_map/ppermute | solution.py:30
  96.1 5.5 %collective-permute-start.1 = (bf16[128,1536]{1,0:T(8,128)(2,1)S(1)}, bf16[128,1536]{1,0:T(8,128)(2,1)S(1)}, u32[]{:S(2)}, u32[]{:S(2)}) collective-permute-start(bf16[128,1536]{1,0:T(8,128)(2,1)S(1)} %get-tuple-element.19), channel_id=1, source_target_pairs={{0,16},{16,0},{1,17},{17,1},{2,18},{18,2},{3,19},{19,3},{4,20},{20... | collective-permute-start | bytes 1179656 | tf_op jit(solution)/shard_map/ppermute | solution.py:30
  98.2 3.3 %collective-permute-start = (bf16[256,384]{1,0:T(8,128)(2,1)S(1)}, bf16[256,384]{1,0:T(8,128)(2,1)S(1)}, u32[]{:S(2)}, u32[]{:S(2)}) collective-permute-start(bf16[256,384]{1,0:T(8,128)(2,1)S(1)} %dynamic-slice_bitcast_fusion), channel_id=1, source_target_pairs={{0,16},{16,0},{1,17},{17,1},{2,18},{18,2},{3,19},{19,3},{4,20},{20... | collective-permute-start | bytes 589832 | tf_op jit(solution)/shard_map/ppermute | solution.py:30

commit v9 on v8

--- a/solution.py
+++ b/solution.py
@@ -49,7 +49,11 @@
     for at in range(others):
         first = (6, 4)[at // (others // 2)]
         groups.append(
-            [(section * chips + (turn + first) % chips) * others + at for section in range(2) for turn in range(chips)]
+            [
+                (section * chips + (first + (turn // 2 if turn % 2 == 0 else -(turn + 1) // 2)) % chips) * others + at
+                for section in range(2)
+                for turn in range(chips)
+            ]
         )
     return lax.all_to_all(blocks, every_axis, 0, 0, axis_index_groups=groups)
 

time: 105 us -> 104 us (level)
  blocking collectives: 58.5 us -> 57.3 us
    all_to_all x2, blocking collectives: 51.5 us -> 50.3 us  [over_rows(): return lax.all_to_all(blocks, every_axis, 0, 0, axis_index_groups=groups)]
where the time goes in v9:
time: 104 us
  blocking collectives  57.3 us (55%)
  starting transfers between devices  34.9 us (34%)
  matrix products  4.32 us (4%)
  local copies, waits for them, and re-layouts  3.13 us (3%)
  waiting for transfers between devices  2.5 us (2%)
    all_to_all x2, blocking collectives, over_rows(): return lax.all_to_all(blocks, every_axis, 0, 0, axis_index_groups=groups)  50.3 us
    all_to_all x2, starting transfers between devices, over_cols(): return lax.all_to_all(blocks, every_axis, 0, 0, axis_index_groups=groups)  28.3 us
    all_gather x3, blocking collectives, per_device(): lax.all_gather(weight[at * step:(at + 1) * step], 'core')  7.08 us
    ppermute x3, starting transfers between devices, swap(): return lax.ppermute(block, axis, [(0, 1), (1, 0)])  6.58 us
  transfers between devices with their start and end apart: 5, of which 3 were waited for; matrix products, arithmetic and copies ran while one was open for 3% of the time, Pallas kernels for 0%

profile of v9, /device:TPU:1, one launch (start us, length us, event | category | flops | bytes accessed | tf_op | source)
XLA Modules:
  0.0 103.9 jit_solution(7606920358932433897)
XLA Ops:
  0.6 1.5 %broadcast_in_dim.11 = bf16[2,16,16,384]{3,2,1,0:T(8,128)(2,1)} broadcast(bf16[2,16,384]{2,1,0:T(8,128)(2,1)} %bitcast.38), dimensions={0,2,3} | broadcast | bytes 417792 | tf_op jit(solution)/shard_map/broadcast_in_dim | solution.py:80
  2.2 16.5 %all-to-all-start = ((bf16[32,16,384]{2,1,0:T(8,128)(2,1)}), bf16[32,16,384]{2,1,0:T(8,128)(2,1)S(1)}, u32[]{:S(2)}, u32[]{:S(2)}) async-start(bf16[32,16,384]{2,1,0:T(8,128)(2,1)} %bitcast.2), calls=%async_computation | async-start | bytes 786432 | tf_op jit(solution)/shard_map/all_to_all | solution.py:67
  18.6 1.3 %fusion.17 = (bf16[1,128,1536]{2,1,0:T(8,128)(2,1)S(1)}, bf16[1,128,1536]{2,1,0:T(8,128)(2,1)S(1)}, bf16[1,128,1536]{2,1,0:T(8,128)(2,1)S(1)}) fusion(bf16[1,384,1536]{2,1,0:T(8,128)(2,1)} %param.3), kind=kLoop, calls=%fused_computation.31 | loop fusion | bytes 2359296 | tf_op jit(solution)/shard_map/slice | solution.py:83
  19.9 2.4 %all_gather.12 = bf16[2,128,1536]{2,1,0:T(8,128)(2,1)S(1)} all-gather(bf16[1,128,1536]{2,1,0:T(8,128)(2,1)S(1)} %get-tuple-element.17), channel_id=1, replica_groups=mesh['section'=2,'y'=8,'core'=2,'z'=8,'x_hi'=2] {'core'}, dimensions={0}, use_global_device_ids=true | all-gather | bytes 1179648 | tf_op jit(solution)/shard_map/all_gather | solution.py:83
  22.3 2.4 %all_gather.13 = bf16[2,128,1536]{2,1,0:T(8,128)(2,1)S(1)} all-gather(bf16[1,128,1536]{2,1,0:T(8,128)(2,1)S(1)} %get-tuple-element.18), channel_id=1, replica_groups=mesh['section'=2,'y'=8,'core'=2,'z'=8,'x_hi'=2] {'core'}, dimensions={0}, use_global_device_ids=true | all-gather | bytes 1179648 | tf_op jit(solution)/shard_map/all_gather | solution.py:83
  24.7 2.4 %all_gather.14 = bf16[2,128,1536]{2,1,0:T(8,128)(2,1)S(1)} all-gather(bf16[1,128,1536]{2,1,0:T(8,128)(2,1)S(1)} %get-tuple-element.16), channel_id=1, replica_groups=mesh['section'=2,'y'=8,'core'=2,'z'=8,'x_hi'=2] {'core'}, dimensions={0}, use_global_device_ids=true | all-gather | bytes 1179648 | tf_op jit(solution)/shard_map/all_gather | solution.py:83
  27.0 0.1 constant_dynamic-update-slice_fusion.2
  27.1 0.1 constant_dynamic-update-slice_fusion.1
  27.1 0.1 constant_dynamic-update-slice_fusion
  27.2 1.3 %all-to-all-done = bf16[32,16,384]{2,1,0:T(8,128)(2,1)S(1)} async-done(((bf16[32,16,384]{2,1,0:T(8,128)(2,1)}), bf16[32,16,384]{2,1,0:T(8,128)(2,1)S(1)}, u32[]{:S(2)}, u32[]{:S(2)}) %all-to-all-start) | async-done | bytes 393248 | tf_op jit(solution)/shard_map/all_to_all | solution.py:67
  28.5 0.8 fusion.1
  29.3 25.6 %all_to_all.20 = bf16[16,16,1536]{2,1,0:T(8,128)(2,1)S(1)} all-to-all(bf16[16,16,1536]{2,1,0:T(8,128)(2,1)S(1)} %bitcast.37), channel_id=1, replica_groups={{192,160,224,128,0,96,32,64,448,416,480,384,256,352,288,320},{193,161,2..., dimensions={0} | all-to-all | bytes 1572864 | tf_op jit(solution)/shard_map/all_to_all | solution.py:58
  54.9 0.1 convert_reduce_fusion
  55.0 0.1 slice_reduce_fusion
  55.0 0.1 fusion.14
  55.2 0.1 pad_maximum_fusion
  55.3 24.6 %all_to_all.21 = bf16[16,16,1536]{2,1,0:T(8,128)(2,1)S(1)} all-to-all(bf16[16,16,1536]{2,1,0:T(8,128)(2,1)S(1)} %pad_maximum_fusion), channel_id=1, replica_groups={{192,160,224,128,0,96,32,64,448,416,480,384,256,352,288,320},{193,161,2..., dimensions={0} | all-to-all | bytes 1572864 | tf_op jit(solution)/shard_map/all_to_all | solution.py:58
  79.9 1.5 %convolution_convert_fusion = bf16[2,384,256]{1,2,0:T(8,128)(2,1)} fusion(bf16[2,384,1536]{2,1,0:T(8,128)(2,1)S(1)} %constant_dynamic-update-slice_fusion, bf16[256,1536,1]{1,0,2:T(8,128)(2,1)S(1)} %bitcast.30), kind=kOutput, calls=%fused_computation.4 | convolution fusion | flops 604176384 | bytes 3538944 | tf_op jit(solution)/shard_map/dot_general | solution.py:94
  81.4 11.9 %all-to-all-start.3 = ((bf16[32,16,384]{2,1,0:T(8,128)(2,1)}), bf16[32,16,384]{2,1,0:T(8,128)(2,1)S(1)}, u32[]{:S(2)}, u32[]{:S(2)}) async-start(bf16[32,16,384]{2,1,0:T(8,128)(2,1)} %bitcast.9), calls=%async_computation.3 | async-start | bytes 786432 | tf_op jit(solution)/shard_map/all_to_all | solution.py:67
  93.3 0.1 fusion.18
  93.4 2.3 %collective-permute-start.2 = (bf16[128,1536]{1,0:T(8,128)(2,1)S(1)}, bf16[128,1536]{1,0:T(8,128)(2,1)S(1)}, u32[]{:S(2)}, u32[]{:S(2)}) collective-permute-start(bf16[128,1536]{1,0:T(8,128)(2,1)S(1)} %get-tuple-element.20), channel_id=1, source_target_pairs={{0,16},{16,0},{1,17},{17,1},{2,18},{18,2},{3,19},{19,3},{4,20},{20... | collective-permute-start | bytes 1179656 | tf_op jit(solution)/shard_map/ppermute | solution.py:30
  95.6 2.1 %collective-permute-start.1 = (bf16[128,1536]{1,0:T(8,128)(2,1)S(1)}, bf16[128,1536]{1,0:T(8,128)(2,1)S(1)}, u32[]{:S(2)}, u32[]{:S(2)}) collective-permute-start(bf16[128,1536]{1,0:T(8,128)(2,1)S(1)} %get-tuple-element.19), channel_id=1, source_target_pairs={{0,16},{16,0},{1,17},{17,1},{2,18},{18,2},{3,19},{19,3},{4,20},{20... | collective-permute-start | bytes 1179656 | tf_op jit(solution)/shard_map/ppermute | solution.py:30
  97.8 2.3 %collective-permute-start = (bf16[256,384]{1,0:T(8,128)(2,1)S(1)}, bf16[256,384]{1,0:T(8,128)(2,1)S(1)}, u32[]{:S(2)}, u32[]{:S(2)}) collective-permute-start(bf16[256,384]{1,0:T(8,128)(2,1)S(1)} %dynamic-slice_bitcast_fusion), channel_id=1, source_target_pairs={{0,16},{16,0},{1,17},{17,1},{2,18},{18,2},{3,19},{19,3},{4,20},{20... | collective-permute-start | bytes 589832 | tf_op jit(solution)/shard_map/ppermute | solution.py:30
  100.0 0.5 fusion.5
  100.5 0.6 collective-permute-done
  101.1 0.0 collective-permute-done.2
  101.1 0.0 collective-permute-done.1
  101.1 1.5 %fusion = bf16[384,1536]{1,0:T(8,128)(2,1)} fusion(f32[384,1536]{1,0:T(8,128)S(1)} %fusion.5, bf16[256,384]{1,0:T(8,128)(2,1)S(1)} %collective-permute-done, bf16[128,1536]{1,0:T(8,128)(2,1)S(1)} %collective-permute-done.2, bf16[128,1536]{1,0:T(8,128)(2,1)S(1)} %collective-permute-done.1), kind=kOutput, calls=%fused_computation.1 | convolution fusion | flops 304742400 | bytes 4521984 | tf_op jit(solution)/shard_map/dot_general | solution.py:42
  102.6 0.6 all-to-all-done.3
  103.2 0.7 bitcast_reduce_fusion
  (3 shorter events, 0.1 us)
Async XLA Ops:
  2.2 26.4 %all-to-all-start = ((bf16[32,16,384]{2,1,0:T(8,128)(2,1)}), bf16[32,16,384]{2,1,0:T(8,128)(2,1)S(1)}, u32[]{:S(2)}, u32[]{:S(2)}) async-start(bf16[32,16,384]{2,1,0:T(8,128)(2,1)} %bitcast.2), calls=%async_computation | async-start | bytes 786432 | tf_op jit(solution)/shard_map/all_to_all | solution.py:67
  81.4 21.8 %all-to-all-start.3 = ((bf16[32,16,384]{2,1,0:T(8,128)(2,1)}), bf16[32,16,384]{2,1,0:T(8,128)(2,1)S(1)}, u32[]{:S(2)}, u32[]{:S(2)}) async-start(bf16[32,16,384]{2,1,0:T(8,128)(2,1)} %bitcast.9), calls=%async_computation.3 | async-start | bytes 786432 | tf_op jit(solution)/shard_map/all_to_all | solution.py:67
  93.4 7.7 %collective-permute-start.2 = (bf16[128,1536]{1,0:T(8,128)(2,1)S(1)}, bf16[128,1536]{1,0:T(8,128)(2,1)S(1)}, u32[]{:S(2)}, u32[]{:S(2)}) collective-permute-start(bf16[128,1536]{1,0:T(8,128)(2,1)S(1)} %get-tuple-element.20), channel_id=1, source_target_pairs={{0,16},{16,0},{1,17},{17,1},{2,18},{18,2},{3,19},{19,3},{4,20},{20... | collective-permute-start | bytes 1179656 | tf_op jit(solution)/shard_map/ppermute | solution.py:30
  95.6 5.5 %collective-permute-start.1 = (bf16[128,1536]{1,0:T(8,128)(2,1)S(1)}, bf16[128,1536]{1,0:T(8,128)(2,1)S(1)}, u32[]{:S(2)}, u32[]{:S(2)}) collective-permute-start(bf16[128,1536]{1,0:T(8,128)(2,1)S(1)} %get-tuple-element.19), channel_id=1, source_target_pairs={{0,16},{16,0},{1,17},{17,1},{2,18},{18,2},{3,19},{19,3},{4,20},{20... | collective-permute-start | bytes 1179656 | tf_op jit(solution)/shard_map/ppermute | solution.py:30
  97.8 3.3 %collective-permute-start = (bf16[256,384]{1,0:T(8,128)(2,1)S(1)}, bf16[256,384]{1,0:T(8,128)(2,1)S(1)}, u32[]{:S(2)}, u32[]{:S(2)}) collective-permute-start(bf16[256,384]{1,0:T(8,128)(2,1)S(1)} %dynamic-slice_bitcast_fusion), channel_id=1, source_target_pairs={{0,16},{16,0},{1,17},{17,1},{2,18},{18,2},{3,19},{19,3},{4,20},{20... | collective-permute-start | bytes 589832 | tf_op jit(solution)/shard_map/ppermute | solution.py:30

commit v10 on v8

--- a/solution.py
+++ b/solution.py
@@ -57,7 +57,7 @@
 def over_cols(blocks):
     deep = lax.axis_size("z")
     across = deep * 2
-    order = [(core * deep + (at + 5) % deep) * 2 + (side + 1) % 2 for core in range(2) for at in range(deep) for side in range(2)]
+    order = [core * across + (at + 11) % across for core in range(2) for at in range(across)]
     chips = lax.axis_size("section") * lax.axis_size("y")
     groups = [[chip * 2 * across + at for at in order] for chip in range(chips)]
     return lax.all_to_all(blocks, every_axis, 0, 0, axis_index_groups=groups)

time: 105 us -> 105 us (level)
  no operation moved by 1% of the time
where the time goes in v10:
time: 105 us; the launch traced here: 104 us
  blocking collectives  58.9 us (56%)
  starting transfers between devices  33.9 us (32%)
  matrix products  4.33 us (4%)
  local copies, waits for them, and re-layouts  3.13 us (3%)
  waiting for transfers between devices  2.54 us (2%)
    all_to_all x2, blocking collectives, over_rows(): return lax.all_to_all(blocks, every_axis, 0, 0, axis_index_groups=groups)  51.8 us
    all_to_all x2, starting transfers between devices, over_cols(): return lax.all_to_all(blocks, every_axis, 0, 0, axis_index_groups=groups)  27.3 us
    all_gather x3, blocking collectives, per_device(): lax.all_gather(weight[at * step:(at + 1) * step], 'core')  7.08 us
    ppermute x3, starting transfers between devices, swap(): return lax.ppermute(block, axis, [(0, 1), (1, 0)])  6.59 us
  transfers between devices with their start and end apart: 5, of which 3 were waited for; matrix products, arithmetic and copies ran while one was open for 3% of the time, Pallas kernels for 0%

profile of v10, /device:TPU:1, one launch (start us, length us, event | category | flops | bytes accessed | tf_op | source)
XLA Modules:
  0.0 104.5 jit_solution(10686369080254563250)
XLA Ops:
  0.6 1.5 %broadcast_in_dim.11 = bf16[2,16,16,384]{3,2,1,0:T(8,128)(2,1)} broadcast(bf16[2,16,384]{2,1,0:T(8,128)(2,1)} %bitcast.38), dimensions={0,2,3} | broadcast | bytes 417792 | tf_op jit(solution)/shard_map/broadcast_in_dim | solution.py:76
  2.2 16.4 %all-to-all-start = ((bf16[32,16,384]{2,1,0:T(8,128)(2,1)}), bf16[32,16,384]{2,1,0:T(8,128)(2,1)S(1)}, u32[]{:S(2)}, u32[]{:S(2)}) async-start(bf16[32,16,384]{2,1,0:T(8,128)(2,1)} %bitcast.2), calls=%async_computation | async-start | bytes 786432 | tf_op jit(solution)/shard_map/all_to_all | solution.py:63
  18.6 1.3 %fusion.17 = (bf16[1,128,1536]{2,1,0:T(8,128)(2,1)S(1)}, bf16[1,128,1536]{2,1,0:T(8,128)(2,1)S(1)}, bf16[1,128,1536]{2,1,0:T(8,128)(2,1)S(1)}) fusion(bf16[1,384,1536]{2,1,0:T(8,128)(2,1)} %param.3), kind=kLoop, calls=%fused_computation.31 | loop fusion | bytes 2359296 | tf_op jit(solution)/shard_map/slice | solution.py:79
  19.9 2.4 %all_gather.12 = bf16[2,128,1536]{2,1,0:T(8,128)(2,1)S(1)} all-gather(bf16[1,128,1536]{2,1,0:T(8,128)(2,1)S(1)} %get-tuple-element.17), channel_id=1, replica_groups=mesh['section'=2,'y'=8,'core'=2,'z'=8,'x_hi'=2] {'core'}, dimensions={0}, use_global_device_ids=true | all-gather | bytes 1179648 | tf_op jit(solution)/shard_map/all_gather | solution.py:79
  22.3 2.4 %all_gather.13 = bf16[2,128,1536]{2,1,0:T(8,128)(2,1)S(1)} all-gather(bf16[1,128,1536]{2,1,0:T(8,128)(2,1)S(1)} %get-tuple-element.18), channel_id=1, replica_groups=mesh['section'=2,'y'=8,'core'=2,'z'=8,'x_hi'=2] {'core'}, dimensions={0}, use_global_device_ids=true | all-gather | bytes 1179648 | tf_op jit(solution)/shard_map/all_gather | solution.py:79
  24.6 2.4 %all_gather.14 = bf16[2,128,1536]{2,1,0:T(8,128)(2,1)S(1)} all-gather(bf16[1,128,1536]{2,1,0:T(8,128)(2,1)S(1)} %get-tuple-element.16), channel_id=1, replica_groups=mesh['section'=2,'y'=8,'core'=2,'z'=8,'x_hi'=2] {'core'}, dimensions={0}, use_global_device_ids=true | all-gather | bytes 1179648 | tf_op jit(solution)/shard_map/all_gather | solution.py:79
  27.0 0.1 constant_dynamic-update-slice_fusion.2
  27.1 0.1 constant_dynamic-update-slice_fusion.1
  27.1 0.1 constant_dynamic-update-slice_fusion
  27.2 1.3 %all-to-all-done = bf16[32,16,384]{2,1,0:T(8,128)(2,1)S(1)} async-done(((bf16[32,16,384]{2,1,0:T(8,128)(2,1)}), bf16[32,16,384]{2,1,0:T(8,128)(2,1)S(1)}, u32[]{:S(2)}, u32[]{:S(2)}) %all-to-all-start) | async-done | bytes 393248 | tf_op jit(solution)/shard_map/all_to_all | solution.py:63
  28.5 0.8 fusion.1
  29.3 26.4 %all_to_all.20 = bf16[16,16,1536]{2,1,0:T(8,128)(2,1)S(1)} all-to-all(bf16[16,16,1536]{2,1,0:T(8,128)(2,1)S(1)} %bitcast.37), channel_id=1, replica_groups={{192,224,0,32,64,96,128,160,448,480,256,288,320,352,384,416},{193,225,1..., dimensions={0} | all-to-all | bytes 1572864 | tf_op jit(solution)/shard_map/all_to_all | solution.py:54
  55.7 0.1 convert_reduce_fusion
  55.8 0.1 slice_reduce_fusion
  55.9 0.1 fusion.14
  56.0 0.1 pad_maximum_fusion
  56.1 25.3 %all_to_all.21 = bf16[16,16,1536]{2,1,0:T(8,128)(2,1)S(1)} all-to-all(bf16[16,16,1536]{2,1,0:T(8,128)(2,1)S(1)} %pad_maximum_fusion), channel_id=1, replica_groups={{192,224,0,32,64,96,128,160,448,480,256,288,320,352,384,416},{193,225,1..., dimensions={0} | all-to-all | bytes 1572864 | tf_op jit(solution)/shard_map/all_to_all | solution.py:54
  81.4 1.6 %convolution_convert_fusion = bf16[2,384,256]{1,2,0:T(8,128)(2,1)} fusion(bf16[2,384,1536]{2,1,0:T(8,128)(2,1)S(1)} %constant_dynamic-update-slice_fusion, bf16[256,1536,1]{1,0,2:T(8,128)(2,1)S(1)} %bitcast.30), kind=kOutput, calls=%fused_computation.4 | convolution fusion | flops 604176384 | bytes 3538944 | tf_op jit(solution)/shard_map/dot_general | solution.py:90
  83.0 10.9 %all-to-all-start.3 = ((bf16[32,16,384]{2,1,0:T(8,128)(2,1)}), bf16[32,16,384]{2,1,0:T(8,128)(2,1)S(1)}, u32[]{:S(2)}, u32[]{:S(2)}) async-start(bf16[32,16,384]{2,1,0:T(8,128)(2,1)} %bitcast.9), calls=%async_computation.3 | async-start | bytes 786432 | tf_op jit(solution)/shard_map/all_to_all | solution.py:63
  93.9 0.1 fusion.18
  94.0 2.3 %collective-permute-start.2 = (bf16[128,1536]{1,0:T(8,128)(2,1)S(1)}, bf16[128,1536]{1,0:T(8,128)(2,1)S(1)}, u32[]{:S(2)}, u32[]{:S(2)}) collective-permute-start(bf16[128,1536]{1,0:T(8,128)(2,1)S(1)} %get-tuple-element.20), channel_id=1, source_target_pairs={{0,16},{16,0},{1,17},{17,1},{2,18},{18,2},{3,19},{19,3},{4,20},{20... | collective-permute-start | bytes 1179656 | tf_op jit(solution)/shard_map/ppermute | solution.py:30
  96.2 2.1 %collective-permute-start.1 = (bf16[128,1536]{1,0:T(8,128)(2,1)S(1)}, bf16[128,1536]{1,0:T(8,128)(2,1)S(1)}, u32[]{:S(2)}, u32[]{:S(2)}) collective-permute-start(bf16[128,1536]{1,0:T(8,128)(2,1)S(1)} %get-tuple-element.19), channel_id=1, source_target_pairs={{0,16},{16,0},{1,17},{17,1},{2,18},{18,2},{3,19},{19,3},{4,20},{20... | collective-permute-start | bytes 1179656 | tf_op jit(solution)/shard_map/ppermute | solution.py:30
  98.3 2.3 %collective-permute-start = (bf16[256,384]{1,0:T(8,128)(2,1)S(1)}, bf16[256,384]{1,0:T(8,128)(2,1)S(1)}, u32[]{:S(2)}, u32[]{:S(2)}) collective-permute-start(bf16[256,384]{1,0:T(8,128)(2,1)S(1)} %dynamic-slice_bitcast_fusion), channel_id=1, source_target_pairs={{0,16},{16,0},{1,17},{17,1},{2,18},{18,2},{3,19},{19,3},{4,20},{20... | collective-permute-start | bytes 589832 | tf_op jit(solution)/shard_map/ppermute | solution.py:30
  100.6 0.5 fusion.5
  101.1 0.6 collective-permute-done
  101.7 0.0 collective-permute-done.2
  101.7 0.0 collective-permute-done.1
  101.7 1.5 %fusion = bf16[384,1536]{1,0:T(8,128)(2,1)} fusion(f32[384,1536]{1,0:T(8,128)S(1)} %fusion.5, bf16[256,384]{1,0:T(8,128)(2,1)S(1)} %collective-permute-done, bf16[128,1536]{1,0:T(8,128)(2,1)S(1)} %collective-permute-done.2, bf16[128,1536]{1,0:T(8,128)(2,1)S(1)} %collective-permute-done.1), kind=kOutput, calls=%fused_computation.1 | convolution fusion | flops 304742400 | bytes 4521984 | tf_op jit(solution)/shard_map/dot_general | solution.py:42
  103.2 0.6 all-to-all-done.3
  103.8 0.7 bitcast_reduce_fusion
  (3 shorter events, 0.1 us)
Async XLA Ops:
  2.2 26.4 %all-to-all-start = ((bf16[32,16,384]{2,1,0:T(8,128)(2,1)}), bf16[32,16,384]{2,1,0:T(8,128)(2,1)S(1)}, u32[]{:S(2)}, u32[]{:S(2)}) async-start(bf16[32,16,384]{2,1,0:T(8,128)(2,1)} %bitcast.2), calls=%async_computation | async-start | bytes 786432 | tf_op jit(solution)/shard_map/all_to_all | solution.py:63
  83.0 20.8 %all-to-all-start.3 = ((bf16[32,16,384]{2,1,0:T(8,128)(2,1)}), bf16[32,16,384]{2,1,0:T(8,128)(2,1)S(1)}, u32[]{:S(2)}, u32[]{:S(2)}) async-start(bf16[32,16,384]{2,1,0:T(8,128)(2,1)} %bitcast.9), calls=%async_computation.3 | async-start | bytes 786432 | tf_op jit(solution)/shard_map/all_to_all | solution.py:63
  94.0 7.7 %collective-permute-start.2 = (bf16[128,1536]{1,0:T(8,128)(2,1)S(1)}, bf16[128,1536]{1,0:T(8,128)(2,1)S(1)}, u32[]{:S(2)}, u32[]{:S(2)}) collective-permute-start(bf16[128,1536]{1,0:T(8,128)(2,1)S(1)} %get-tuple-element.20), channel_id=1, source_target_pairs={{0,16},{16,0},{1,17},{17,1},{2,18},{18,2},{3,19},{19,3},{4,20},{20... | collective-permute-start | bytes 1179656 | tf_op jit(solution)/shard_map/ppermute | solution.py:30
  96.2 5.4 %collective-permute-start.1 = (bf16[128,1536]{1,0:T(8,128)(2,1)S(1)}, bf16[128,1536]{1,0:T(8,128)(2,1)S(1)}, u32[]{:S(2)}, u32[]{:S(2)}) collective-permute-start(bf16[128,1536]{1,0:T(8,128)(2,1)S(1)} %get-tuple-element.19), channel_id=1, source_target_pairs={{0,16},{16,0},{1,17},{17,1},{2,18},{18,2},{3,19},{19,3},{4,20},{20... | collective-permute-start | bytes 1179656 | tf_op jit(solution)/shard_map/ppermute | solution.py:30
  98.3 3.3 %collective-permute-start = (bf16[256,384]{1,0:T(8,128)(2,1)S(1)}, bf16[256,384]{1,0:T(8,128)(2,1)S(1)}, u32[]{:S(2)}, u32[]{:S(2)}) collective-permute-start(bf16[256,384]{1,0:T(8,128)(2,1)S(1)} %dynamic-slice_bitcast_fusion), channel_id=1, source_target_pairs={{0,16},{16,0},{1,17},{17,1},{2,18},{18,2},{3,19},{19,3},{4,20},{20... | collective-permute-start | bytes 589832 | tf_op jit(solution)/shard_map/ppermute | solution.py:30
